TPU v7x, 256 devices: a whole 4x4x8 slice. The times are simulated.
256 devices in a mesh: ia: 8 (over x_hi, y), ja: 4 (over x_lo, core), vert: 8 (over z).
Axes of the slice: x: 4 (x_hi: 2, x_lo: 2; x = x_hi * 2 + x_lo), y: 4, z: 8, core: 2. Of those that a mesh axis runs over, the one named last changes fastest.
Arguments:
- amplitudes: bfloat16 [80, 80, 4096], P('ia', 'ja', 'vert'), may hold values from -6 to 6
- ladder_w: bfloat16 [80, 80, 6400], P('ia', 'ja'), may hold values from -0.078125 to 0.078125
- ph_left: bfloat16 [80, 512, 5120], P('ia', 'vert'), may hold values from -6 to 6
- ph_right: bfloat16 [80, 512, 5120], P('ia', 'vert', 'ja'), may hold values from -0.03125 to 0.03125
- occ_sym: int32 [80], replicated, may hold values from 0 to 7
- vir_sym: int32 [64], replicated, may hold values from 0 to 7
Outputs:
- residual: bfloat16 [80, 80, 4096], P('ia', 'ja', 'vert')
Inputs may be any that keep to these rules, and one draw needn't show every extreme that they name: `occ_sym`: D2h irrep labels, combined by bitwise xor. `vir_sym`: D2h irrep labels, combined by bitwise xor.
All inputs are finite; a program needn't handle non-finite values.
Results may differ from a plain program's by a relative error of at most 0.001.
Values may be sent and summed in bfloat16 or wider, within the bound.
No kernel may reach another device: no remote copies, remote signals or barrier semaphores. Data moves between devices by JAX's collectives and lax.ppermute only.
A program may use at most 192 MiB of HBM per device.

v0:
```python
import jax
import jax.numpy as jnp
from jax import lax
from jax.sharding import PartitionSpec as P


def body(amplitudes, ladder_w, ph_left, ph_right, occ_sym, vir_sym):
    rows_i = ph_left.shape[0]
    local_c = ph_left.shape[1]
    slab = vir_sym.shape[0]
    occ_all = ph_left.shape[2] // slab
    cols_j = ph_right.shape[2] // slab
    blocks = lax.axis_size("vert")
    rows_a = slab // blocks
    left_view = ph_left.reshape(rows_i, local_c, occ_all, slab)
    piece = lax.all_gather(ph_right, "ia", axis=0, tiled=True)
    right_part = piece.reshape(piece.shape[0], local_c, cols_j, slab)
    partial_value = jnp.einsum(
        "icka,kcjb->ijab", left_view, right_part, preferred_element_type=jnp.float32
    )
    total = lax.psum(partial_value, "vert")
    anti_full = total - jnp.swapaxes(total, 2, 3)
    anti = lax.dynamic_slice_in_dim(anti_full, lax.axis_index("vert") * rows_a, rows_a, 2)
    anti = anti.reshape(rows_i, cols_j, rows_a * slab)
    columns = lax.all_gather(amplitudes, "ja", axis=1, tiled=True)
    weight_view = ladder_w.reshape(rows_i, cols_j, occ_all, occ_all)
    ladder = jnp.einsum(
        "ijkl,klp->ijp",
        weight_view,
        lax.all_gather(columns, "ia", axis=0, tiled=True),
        preferred_element_type=jnp.float32,
    )
    sym_i = lax.dynamic_slice_in_dim(occ_sym, lax.axis_index("ia") * rows_i, rows_i, 0)
    sym_j = lax.dynamic_slice_in_dim(occ_sym, lax.axis_index("ja") * cols_j, cols_j, 0)
    sym_a = lax.dynamic_slice_in_dim(vir_sym, lax.axis_index("vert") * rows_a, rows_a, 0)
    sym_ij = jnp.bitwise_xor(sym_i[:, None], sym_j[None, :])
    sym_ab = jnp.bitwise_xor(sym_a[:, None], vir_sym[None, :]).reshape(rows_a * slab)
    mask = (jnp.bitwise_xor(sym_ij[:, :, None], sym_ab[None, None, :]) == 0).astype(jnp.float32)
    return (mask * (anti + ladder)).astype(jnp.bfloat16)


def solution(mesh):
    in_specs = (
        P("ia", "ja", "vert"),
        P("ia", "ja", None),
        P("ia", "vert", None),
        P("ia", "vert", "ja"),
        P(),
        P(),
    )
    out_specs = P("ia", "ja", "vert")
    return jax.shard_map(body, mesh=mesh, in_specs=in_specs, out_specs=out_specs, check_vma=False)
```

profile of v0, /device:TPU:1, one launch (start us, length us, event | category | flops | bytes accessed | tf_op | source)
XLA Modules:
  0.0 486.3 jit_solution(16473437660726959338)
XLA Ops:
  6.5 0.7 all-gather.3.cloned.1.call-update
  7.3 16.3 %reshape.56 = bf16[10,64,80,64]{3,2,1,0:T(8,128)(2,1)} reshape(bf16[10,64,5120]{2,1,0:T(8,128)(2,1)} %param.8) | data formatting | bytes 13107200 | tf_op jit(solution)/shard_map/reshape | solution.py:15
  23.6 144.5 %all-gather.3.cloned.1.call-done = bf16[80,64,1280]{2,1,0:T(8,128)(2,1)} async-done(((bf16[10,64,1280]{2,1,0:T(8,128)(2,1)}), bf16[80,64,1280]{2,1,0:T(8,128)(2,1)}) %all-gather.3.cloned.1.call-update) | async-done | bytes 13107216 | tf_op jit(solution)/shard_map/all_gather | solution.py:16
  168.1 26.3 %copy.16 = bf16[80,64,1280]{0,2,1:T(8,128)(2,1)} copy(bf16[80,64,1280]{2,1,0:T(8,128)(2,1)} %all-gather.3.cloned.1.call-done) | data formatting | bytes 26214400 | tf_op jit(solution)/shard_map/all_gather | solution.py:16
  194.4 28.8 %fusion.6 = f32[10,20,64,64]{2,3,0,1:T(8,128)} fusion(bf16[10,64,80,64]{3,2,1,0:T(8,128)(2,1)} %reshape.56, bf16[80,64,20,64,1]{0,3,2,1,4:T(8,128)(2,1)} %bitcast.37), kind=kOutput, calls=%fused_computation.7 | convolution fusion | flops 8388608000 | bytes 22937600 | tf_op jit(solution)/shard_map/icka,kcjb->ijab/dot_general | solution.py:18
  223.2 0.0 all-gather.5.cloned.1.call-start
  223.3 0.8 copy-done.1
  224.1 0.1 copy.21
  224.2 11.9 %all_gather.10 = bf16[10,80,512]{2,0,1:T(8,128)(2,1)S(1)} all-gather(bf16[10,20,512]{2,0,1:T(8,128)(2,1)S(1)} %copy.21), channel_id=1, replica_groups=mesh['ia'=8,'ja'=4,'vert'=8] {'ja'}, dimensions={1}, use_global_device_ids=true | all-gather | bytes 1024000 | tf_op jit(solution)/shard_map/all_gather | solution.py:25
  236.1 1.3 copy.22
  237.5 0.1 dynamic_slice.12
  237.5 0.1 dynamic_slice.13
  237.6 0.1 dynamic_slice.14
  237.7 0.1 broadcast_xor_fusion.1
  237.8 0.1 xor.57
  237.8 7.8 %reshape.58 = bf16[10,20,80,80]{3,2,1,0:T(8,128)(2,1)} reshape(bf16[10,20,6400]{2,1,0:T(8,128)(2,1)S(1)} %copy-done) | data formatting | bytes 5120000 | tf_op jit(solution)/shard_map/reshape | solution.py:26
  245.7 0.1 broadcast_xor_fusion
  245.7 129.4 %all-reduce.2.cloned.1.call-done = f32[10,20,64,64]{2,3,0,1:T(8,128)} async-done(((f32[10,20,64,64]{2,3,0,1:T(8,128)}), f32[10,20,64,64]{2,3,0,1:T(8,128)}) %all-reduce.2.cloned.1.call-update) | async-done | bytes 3276816 | tf_op jit(solution)/shard_map/psum | solution.py:21
  375.1 8.1 %copy.19 = f32[10,20,64,64]{3,2,0,1:T(8,128)} copy(f32[10,20,64,64]{2,3,0,1:T(8,128)} %all-reduce.2.cloned.1.call-done) | data formatting | bytes 6553600 | tf_op jit(solution)/shard_map/psum | solution.py:21
  383.3 11.0 %dynamic-slice_subtract_fusion = f32[10,20,8,64]{2,3,0,1:T(8,128)} fusion(f32[10,20,64,64]{2,3,0,1:T(8,128)} %bitcast.36, s32[]{:T(128)S(6)} %select_n.12, f32[10,20,64,64]{2,3,0,1:T(8,128)} %all-reduce.2.cloned.1.call-done), kind=kLoop, calls=%fused_computation.3 | loop fusion | flops 102400 | bytes 1228804 | tf_op jit(solution)/shard_map/sub | solution.py:22
  394.2 4.6 copy.20
  398.8 0.2 reshape.57
  399.0 73.2 %all-gather.5.cloned.1.call-done = bf16[80,80,512]{2,1,0:T(8,128)(2,1)} async-done(((bf16[10,80,512]{2,1,0:T(8,128)(2,1)}), bf16[80,80,512]{2,1,0:T(8,128)(2,1)}) %all-gather.5.cloned.1.call-update) | async-done | bytes 6553616 | tf_op jit(solution)/shard_map/all_gather | solution.py:30
  472.2 7.5 %fusion.26 = bf16[10,20,512]{2,1,0:T(8,128)(2,1)} fusion(f32[10,20,512]{2,1,0:T(8,128)S(1)} %reshape.57, bf16[80,80,512]{2,1,0:T(8,128)(2,1)} %all-gather.5.cloned.1.call-done, bf16[10,20,80,80]{3,2,1,0:T(8,128)(2,1)} %reshape.58, s32[512]{0:T(512)S(1)} %xor.57, s32[10,20]{1,0:T(8,128)S(1)} %broadcast_xor_fusion), kind=kOutput, calls=%fused_computation.11 | convolution fusion | flops 1311232000 | bytes 9730848 | tf_op jit(solution)/shard_map/ijkl,klp->ijp/dot_general | solution.py:27
  (11 shorter events, 0.1 us)
Async XLA Ops:
  6.5 161.6 %all-gather.3.cloned.1.call-start = ((), (), s32[]{:S(2)}) async-start(), calls=%async_computation | async-start | bytes 14745600 | tf_op jit(solution)/shard_map/all_gather | solution.py:16
  7.3 367.9 %all-reduce.2.cloned.1.call-start = ((), (), s32[]{:S(2)}) async-start(), calls=%async_computation.1 | async-start | bytes 13107200 | tf_op jit(solution)/shard_map/psum | solution.py:21
  223.2 0.9 copy-start.1
  223.2 14.3 %copy-start.3 = (s32[80]{0:T(128)S(1)}, s32[80]{0:T(128)}, u32[]{:S(2)}) copy-start(s32[80]{0:T(128)} %param.10) | copy-start | bytes 964
  223.2 14.4 %copy-start.2 = (s32[64]{0:T(128)S(1)}, s32[64]{0:T(128)}, u32[]{:S(2)}) copy-start(s32[64]{0:T(128)} %param.11) | copy-start | bytes 772
  223.2 14.7 %copy-start = (bf16[10,20,6400]{2,1,0:T(8,128)(2,1)S(1)}, bf16[10,20,6400]{2,1,0:T(8,128)(2,1)}, u32[]{:S(2)}) copy-start(bf16[10,20,6400]{2,1,0:T(8,128)(2,1)} %param.7) | copy-start | bytes 7680004
  223.2 249.0 %all-gather.5.cloned.1.call-start = ((), (), s32[]{:S(2)}) async-start(), calls=%async_computation.2 | async-start | bytes 7372800 | tf_op jit(solution)/shard_map/all_gather | solution.py:30
Sparse Core Ops, SparseCore 0:
  10.0 158.0 all-gather.2
  223.3 151.7 all-reduce.1
  377.7 94.4 all-gather.4
where the time goes:
time: 488 us; the launch traced here: 486 us
  waiting for transfers between devices  348 us (71%)
  local copies, waits for them, and re-layouts  65.9 us (14%)
  matrix products  36.3 us (7%)
  between operations  13.2 us (3%)
  blocking collectives  11.9 us (2%)
  other arithmetic  11.1 us (2%)
    all_gather x1, waiting for transfers between devices, body(): piece = lax.all_gather(ph_right, 'ia', axis=0, tiled=True)  145 us
    psum x1, waiting for transfers between devices, body(): total = lax.psum(partial_value, 'vert')  129 us
    all_gather x1, waiting for transfers between devices, body(): lax.all_gather(columns, 'ia', axis=0, tiled=True)  73.2 us
    dot_general x1, matrix products, body(): jnp.einsum('icka,kcjb->ijab', left_view, right_part, preferred_element_ty...  28.8 us
    all_gather x1, local copies, waits for them, and re-layouts, body(): piece = lax.all_gather(ph_right, 'ia', axis=0, tiled=True)  26.3 us
    reshape x1, local copies, waits for them, and re-layouts, body(): left_view = ph_left.reshape(rows_i, local_c, occ_all, slab)  16.3 us
    all_gather x1, blocking collectives, body(): columns = lax.all_gather(amplitudes, 'ja', axis=1, tiled=True)  11.9 us
    sub x1, other arithmetic, body(): anti_full = total - jnp.swapaxes(total, 2, 3)  11 us
  transfers between devices with their start and end apart: 3, of which 3 were waited for; matrix products, arithmetic and copies ran while one was open for 10% of the time, Pallas kernels for 0%

commit v1 on v0

v1 whole, which is shorter than its diff:
```python
import functools

import jax
import jax.numpy as jnp
from jax import lax
from jax.experimental import pallas as pl
from jax.experimental.pallas import tpu as pltpu
from jax.sharding import PartitionSpec as P

F32 = jnp.float32
BF16 = jnp.bfloat16
SCALE = 32.0
FIRST = 10


def cost(us):
    return pl.CostEstimate(flops=int(us * 1e9), bytes_accessed=int(us * 3e6), transcendentals=0)


def swap_blocks(tile):
    turned = tile.T
    top, bottom = turned[:64], turned[64:]
    low = lax.broadcasted_iota(jnp.int32, (64, 128), 1) < 64
    return (
        jnp.where(low, top, pltpu.roll(bottom, 64, 1)),
        jnp.where(low, pltpu.roll(top, 64, 1), bottom),
    )


def turn_body(index, u, out):
    for ip in range(u.shape[0] // 2):
        for kp in range(u.shape[2] // 128):
            lanes = slice(128 * kp, 128 * kp + 128)
            tile = jnp.concatenate([u[2 * ip, :, lanes], u[2 * ip + 1, :, lanes]], axis=0)
            first, second = swap_blocks(tile)
            out[128 * ip : 128 * ip + 64, lanes] = first
            out[128 * ip + 64 : 128 * ip + 128, lanes] = second


def turn_slabs(u, index):
    count, size = index.shape[0], u.shape[0] * 64
    return pl.pallas_call(
        turn_body,
        out_shape=jax.ShapeDtypeStruct((size, count * size), BF16),
        grid_spec=pltpu.PrefetchScalarGridSpec(
            num_scalar_prefetch=1,
            grid=(count,),
            in_specs=[pl.BlockSpec((u.shape[0], 64, size), lambda s, index: (0, 0, index[s]))],
            out_specs=pl.BlockSpec((size, size), lambda s, index: (0, s)),
        ),
        compiler_params=pltpu.CompilerParams(vmem_limit_bytes=60 << 20),
        cost_estimate=cost(0.5 * count),
    )(index.astype(jnp.int32), u)


def near_body(place, near, far, v0, v1, v3, out, left, right):
    size = near.shape[0]

    @pl.when(place[0] == 0)
    def _():
        left[...] = near[:, :size]
        right[:size, :] = v1[...]
        right[size : 2 * size, :] = v3[...]

    @pl.when(place[0] != 0)
    def _():
        left[...] = far[:, :size]
        right[:size, :] = v3[...]
        right[size : 2 * size, :] = v1[...]

    for low, high in ((0, 384), (384, 640)):
        total = jnp.dot(near[low:high, size:], right[:size, :], preferred_element_type=F32)
        total += jnp.dot(far[low:high, size:], right[size:, :], preferred_element_type=F32)
        out[low:high, :] = total + jnp.dot(left[low:high, :], v0[...], preferred_element_type=F32)


def product_near(place, left, parts):
    size, width = parts[0].shape
    side = lambda at: pl.BlockSpec((size, 2 * size), lambda s, place: (0, at))
    whole = lambda x: pl.BlockSpec(x.shape, lambda s, place: (0,) * x.ndim)
    out = jax.ShapeDtypeStruct((size, width), F32)
    return pl.pallas_call(
        near_body,
        out_shape=out,
        grid_spec=pltpu.PrefetchScalarGridSpec(
            num_scalar_prefetch=1,
            grid=(1,),
            in_specs=[side(0), side(2 - len(left))] + [whole(x) for x in parts],
            out_specs=whole(out),
            scratch_shapes=[pltpu.VMEM((size, size), BF16), pltpu.VMEM((2 * size, width), BF16)],
        ),
        compiler_params=pltpu.CompilerParams(vmem_limit_bytes=32 << 20),
        cost_estimate=cost(1),
    )(place.astype(jnp.int32).reshape(1), left[0], left[-1], *parts)


def product_body(start, place, partial_sum, near, far, v2a, v2b, out, left):
    size, width = near.shape[0], out.shape[2]
    columns = slice(start, start + width)

    @pl.when(place[0] == 0)
    def _():
        left[...] = far[...]

    @pl.when(place[0] != 0)
    def _():
        left[...] = near[...]

    right = jnp.concatenate([v2a[:, columns], v2b[:, columns]], axis=0)
    for low, high in ((0, 384), (384, 640)):
        total = partial_sum[low:high, columns]
        total += jnp.dot(left[low:high, :], right, preferred_element_type=F32)
        for at in range(low, high, 128):
            for jp in range(width // 128):
                lanes = slice(128 * jp, 128 * jp + 128)
                tile = total[at - low : at - low + 128, lanes]
                first, second = swap_blocks(tile)
                first, second = tile[:64] - first, tile[64:] - second
                for z in range(8):
                    out[z, at // 8 : at // 8 + 8, lanes] = first[8 * z : 8 * z + 8]
                    out[z, at // 8 + 8 : at // 8 + 16, lanes] = second[8 * z : 8 * z + 8]


def product(place, left, partial_sum, parts, start, width):
    size = partial_sum.shape[0]
    side = lambda at: pl.BlockSpec((size, size), lambda s, place: (0, at))
    whole = lambda x: pl.BlockSpec(x.shape, lambda s, place: (0,) * x.ndim)
    out = jax.ShapeDtypeStruct((8, size // 8, width), F32)
    return pl.pallas_call(
        functools.partial(product_body, start),
        out_shape=out,
        grid_spec=pltpu.PrefetchScalarGridSpec(
            num_scalar_prefetch=1,
            grid=(1,),
            in_specs=[whole(partial_sum), side(0), side(2 * (2 - len(left)))]
            + [whole(x) for x in parts],
            out_specs=whole(out),
            scratch_shapes=[pltpu.VMEM((size, size), BF16)],
        ),
        compiler_params=pltpu.CompilerParams(vmem_limit_bytes=24 << 20),
        cost_estimate=cost(1),
    )(place.astype(jnp.int32).reshape(1), partial_sum, left[0], left[-1], *parts)


def ring(n, shift):
    return [(i, (i + shift) % n) for i in range(n)]


def y_ring(shift):
    return [(4 * h + y, 4 * h + (y + shift) % 4) for h in range(2) for y in range(4)]


X_HI = [(i, (i + 4) % 8) for i in range(8)]
CORE = [(j, j ^ 1) for j in range(4)]
X_LO = [(j, j ^ 2) for j in range(4)]
X_CROSS = [(4 * i + j, 4 * ((i + 4) % 8) + (j ^ 2)) for i in range(8) for j in range(4)]


def after(*values):
    return lax.optimization_barrier(values)


def sort_body(w, order, out, rows):
    count = w.shape[1]
    for i in range(w.shape[0]):
        rows[count * i : count * i + count, :] = w[i].astype(F32)
    out[...] = jnp.dot(rows[...].astype(BF16), order[...], preferred_element_type=F32).astype(BF16)


def sort_columns(weights, order):
    rows_i, cols_j, columns = weights.shape
    rows, width = rows_i * cols_j, order.shape[0]
    return pl.pallas_call(
        sort_body,
        out_shape=jax.ShapeDtypeStruct((rows, columns), BF16),
        grid=(columns // width,),
        in_specs=[
            pl.BlockSpec((rows_i, cols_j, width), lambda s: (0, 0, s)),
            pl.BlockSpec((width, width), lambda s: (0, 0)),
        ],
        out_specs=pl.BlockSpec((rows, width), lambda s: (0, s)),
        scratch_shapes=[pltpu.VMEM((rows, width), F32)],
        compiler_params=pltpu.CompilerParams(vmem_limit_bytes=24 << 20),
        cost_estimate=cost(1),
    )(weights, order)


def arrival_order(occ, cols_j):
    width = 8 * occ
    column = jnp.arange(width)
    block, rest = column // (8 * cols_j), column % (8 * cols_j)
    source = (rest // cols_j) * occ + block * cols_j + rest % cols_j
    return (jnp.arange(width)[:, None] == source[None, :]).astype(BF16)


def order_body(start, own, down, two_a, two_b, up, out):
    count = own.shape[0]
    for n in range(count):
        for d, part in ((0, own), (1, down), (3, up)):
            out[n, lax.rem(start[0] + d, 4)] = part[n]
        two = (two_a, two_b)[n // (count // 2)]
        out[n, lax.rem(start[0] + 2, 4)] = two[n % (count // 2)]


def order_pieces(start, pieces):
    whole = lambda x: pl.BlockSpec(x.shape, lambda s, start: (0,) * x.ndim)
    count, rows, width = pieces[0].shape
    out = jax.ShapeDtypeStruct((count, 4, rows, width), BF16)
    return pl.pallas_call(
        order_body,
        out_shape=out,
        grid_spec=pltpu.PrefetchScalarGridSpec(
            num_scalar_prefetch=1,
            grid=(1,),
            in_specs=[whole(x) for x in pieces],
            out_specs=whole(out),
        ),
        compiler_params=pltpu.CompilerParams(vmem_limit_bytes=16 << 20),
        cost_estimate=cost(0.5),
    )(start.astype(jnp.int32).reshape(1), *pieces).reshape(count, 4 * rows, width)


def ladder_body(place, w, near, far, out, full):
    run = near.shape[1] // 5
    for half in range(2):
        for block in range(4):
            x = (half ^ place[0]) * 2 + ((block // 2) ^ place[1])
            for group in range(5):
                at = (half * 20 + group * 4 + block) * run
                rows = slice(group * run, group * run + run)

                @pl.when(block % 2 == place[2])
                def _():
                    full[at : at + run, :] = near[x, rows, :]

                @pl.when(block % 2 != place[2])
                def _():
                    full[at : at + run, :] = far[x, rows, :]

    rows = out.shape[1]
    total = jnp.dot(w[...], full[...], preferred_element_type=F32)
    for i in range(out.shape[0]):
        out[i] = total[rows * i : rows * i + rows]


def ladder_sum(place, weights, near, far, rows_i):
    whole = lambda x: pl.BlockSpec(x.shape, lambda s, place: (0,) * x.ndim)
    out = jax.ShapeDtypeStruct((rows_i, weights.shape[0] // rows_i, near.shape[2]), F32)
    return pl.pallas_call(
        ladder_body,
        out_shape=out,
        grid_spec=pltpu.PrefetchScalarGridSpec(
            num_scalar_prefetch=1,
            grid=(1,),
            in_specs=[whole(weights), whole(near), whole(far)],
            out_specs=whole(out),
            scratch_shapes=[pltpu.VMEM((weights.shape[1], near.shape[2]), BF16)],
        ),
        compiler_params=pltpu.CompilerParams(vmem_limit_bytes=28 << 20),
        cost_estimate=cost(1),
    )(place.astype(jnp.int32), weights, near, far)


def finish_body(sym_i, sum0, own0, sum1, own1, ladder, table, out, rows):
    low = lax.broadcasted_iota(jnp.int32, (8, 128), 1) < 64
    for i in range(out.shape[0]):
        j = 0
        for part, own in ((sum0, own0), (sum1, own1)):
            for jp in range(part.shape[1] // 128):
                at = slice(8 * i, 8 * i + 8), slice(128 * jp, 128 * jp + 128)
                tile = (part[at] + own[at]) * (1.0 / SCALE)
                turned = pltpu.roll(tile, 64, 1)
                even = jnp.where(low, tile, pltpu.roll(turned, 7, 0))
                odd = jnp.where(low, turned, pltpu.roll(tile, 7, 0))
                for ap in range(4):
                    rows[i, ap, j : j + 1, :] = even[2 * ap : 2 * ap + 1]
                    rows[i, ap, j + 1 : j + 2, :] = odd[2 * ap : 2 * ap + 1]
                j += 2
        for ap in range(4):
            lanes = slice(128 * ap, 128 * ap + 128)
            value = rows[i, ap] + ladder[i, :, lanes]
            out[i, :, lanes] = jnp.where(table[:, lanes] == sym_i[i], value, 0.0).astype(BF16)


def finish(sym_i, sums, ladder, table):
    whole = lambda x: pl.BlockSpec(x.shape, lambda s, sym_i: (0,) * x.ndim)
    rows_i, cols_j, width = ladder.shape
    return pl.pallas_call(
        finish_body,
        out_shape=jax.ShapeDtypeStruct(ladder.shape, BF16),
        grid_spec=pltpu.PrefetchScalarGridSpec(
            num_scalar_prefetch=1,
            grid=(1,),
            in_specs=[whole(x) for x in (*sums, ladder, table)],
            out_specs=whole(ladder),
            scratch_shapes=[pltpu.VMEM((rows_i, width // 128, cols_j, 128), F32)],
        ),
        compiler_params=pltpu.CompilerParams(vmem_limit_bytes=56 << 20),
        cost_estimate=cost(1),
    )(sym_i, *sums, ladder, table)


def body(amplitudes, ladder_w, ph_left, ph_right, occ_sym, vir_sym):
    rows_i, local_c = ph_left.shape[:2]
    slab = vir_sym.shape[0]
    occ = occ_sym.shape[0]
    cols_j = ph_right.shape[2] // slab
    rows_a = slab // 8
    ia, ja, z = lax.axis_index("ia"), lax.axis_index("ja"), lax.axis_index("vert")
    h, y, core = ia // 4, ia % 4, ja % 2
    around = (y + jnp.arange(4)) % 4

    right = ph_right.reshape(rows_i * local_c, cols_j * slab)
    half = rows_i * local_c // 2
    up = lax.ppermute(right, "ia", y_ring(1))
    down = lax.ppermute(right, "ia", y_ring(-1))
    t = amplitudes.reshape(rows_i * cols_j, -1)
    tx = [t, lax.ppermute(t, "ja", X_LO), lax.ppermute(t, "ia", X_HI)]
    tx.append(lax.ppermute(t, ("ia", "ja"), X_CROSS))
    mine = turn_slabs(ph_left, (1 - h) * 4 + jnp.roll(around, -2 * core)[:2])
    got = lax.ppermute(mine, ("ia", "ja"), X_CROSS)
    ph_left, mine = after(ph_left, mine)
    left = turn_slabs(ph_left, h * 4 + around)
    w, left, order = after(ladder_w, left, arrival_order(occ, cols_j))
    weights = sort_columns(w, order)

    up, down, weights = after(up, down, weights)
    v2a = lax.ppermute(up[:half], "ia", y_ring(1))
    v2b = lax.ppermute(down[half:], "ia", y_ring(-1))
    flat = jnp.zeros_like(z)
    ours = product_near(flat, (left,), (right, down, up))
    got, ours = after(got, ours)
    got_core = lax.ppermute(got, "ja", CORE)
    theirs = product_near(core, (got, got_core), (right, down, up))

    theirs, ours, *tx = after(theirs, ours, *tx)
    tx = jnp.stack(tx)
    t_up = lax.ppermute(tx, "ia", y_ring(1))
    t_down = lax.ppermute(tx, "ia", y_ring(-1))

    v2a, v2b, tx = after(v2a, v2b, tx)
    first, rest = FIRST * slab, (cols_j - FIRST) * slab
    theirs0 = product(core, (got, got_core), theirs, (v2a, v2b), 0, first)
    left, theirs0 = after(left, theirs0)
    ours0 = product(flat, (left,), ours, (v2a, v2b), 0, first)
    sent0 = (jnp.concatenate([ours0, theirs0], axis=1) * SCALE).astype(jnp.float16)
    pieces0 = lax.all_to_all(sent0, "vert", 0, 0, tiled=True)

    left, sent0 = after(left, sent0)
    ours1 = product(flat, (left,), ours, (v2a, v2b), first, rest)
    got, ours1 = after(got, ours1)
    theirs1 = product(core, (got, got_core), theirs, (v2a, v2b), first, rest)
    theirs1 = (theirs1 * SCALE).astype(jnp.float16)
    t_up, t_down, theirs1 = after(t_up, t_down, theirs1)
    theirs1 = lax.ppermute(theirs1, "ia", X_HI)
    t_two_a = lax.ppermute(t_up[:2], "ia", y_ring(1))
    t_two_b = lax.ppermute(t_down[2:], "ia", y_ring(-1))
    sent1 = ours1 * SCALE + theirs1.astype(F32)
    sent1_16 = sent1.astype(jnp.float16)
    own1 = lax.dynamic_index_in_dim(sent1, z, 0, keepdims=False)
    own1 -= lax.dynamic_index_in_dim(sent1_16, z, 0, keepdims=False).astype(F32)
    pieces1 = lax.all_to_all(sent1_16, "vert", 0, 0, tiled=True)

    tx, t_down, t_two_a, t_two_b, t_up, sent1_16 = after(tx, t_down, t_two_a, t_two_b, t_up, sent1_16)
    near = order_pieces(y, (tx, t_down, t_two_a, t_two_b, t_up))
    far = lax.ppermute(near, "ja", CORE)

    pieces0, sent1_16, own1, near = after(pieces0, sent1_16, own1, near)
    ladder = ladder_sum(jnp.stack([h, ja // 2, core]), weights, near, far, rows_i)
    sum0 = jnp.sum(pieces0.astype(F32), axis=0)
    size = sum0.shape[0] // 2
    other0 = lax.ppermute(sum0[size:], "ia", X_HI)

    sym_i = lax.dynamic_slice_in_dim(occ_sym, ia * rows_i, rows_i, 0)
    sym_j = lax.dynamic_slice_in_dim(occ_sym, ja * cols_j, cols_j, 0)
    sym_a = lax.dynamic_slice_in_dim(vir_sym, z * rows_a, rows_a, 0)
    sym_ab = jnp.bitwise_xor(sym_a[:, None], vir_sym[None, :]).reshape(rows_a * slab)
    table = jnp.bitwise_xor(sym_j[:, None], sym_ab[None, :])
    pieces1, ladder, other0, table, sym_i = after(pieces1, ladder, other0, table, sym_i)
    sum1 = jnp.sum(pieces1.astype(F32), axis=0)
    return finish(sym_i, (sum0[:size], other0, sum1, own1), ladder, table)


def solution(mesh):
    in_specs = (
        P("ia", "ja", "vert"),
        P("ia", "ja", None),
        P("ia", "vert", None),
        P("ia", "vert", "ja"),
        P(),
        P(),
    )
    out_specs = P("ia", "ja", "vert")
    return jax.shard_map(body, mesh=mesh, in_specs=in_specs, out_specs=out_specs, check_vma=False)
```

time: 488 us -> 178 us (0.36)
  waiting for transfers between devices: 348 us -> 63.6 us
  local copies, waits for them, and re-layouts: 65.9 us -> 16.3 us
  Pallas kernels: 0 us -> 49.3 us
  starting transfers between devices: 0.08 us -> 36.8 us
  matrix products: 36.3 us -> 0 us
  between operations: 13.2 us -> 0.31 us
  blocking collectives: 11.9 us -> 0 us
    all_gather x2 -> x0, waiting for transfers between devices: 218 us -> none  [the longest x1 145 us: body(): piece = lax.all_gather(ph_right, 'ia', axis=0, tiled=True)]
    psum x1 -> x0, waiting for transfers between devices: 129 us -> none  [body(): total = lax.psum(partial_value, 'vert')]
    pallas_call x0 -> x12, Pallas kernels: none -> 49.3 us  [the longest x2 13.5 us: product_near(): pl.pallas_call(near_body, out_shape=out, grid_spec=pltpu.PrefetchScalarGr...]
    all_to_all x0 -> x2, waiting for transfers between devices: none -> 37.8 us  [the longest x1 27.1 us: body(): pieces0 = lax.all_to_all(sent0, 'vert', 0, 0, tiled=True)]
    dot_general x2 -> x0, matrix products: 36.3 us -> none  [the longest x1 28.8 us: body(): jnp.einsum('icka,kcjb->ijab', left_view, right_part, preferred_element_ty...]
    all_gather x2 -> x0, local copies, waits for them, and re-layouts: 27.7 us -> none  [the longest x1 26.3 us: body(): piece = lax.all_gather(ph_right, 'ia', axis=0, tiled=True)]
    ppermute x0 -> x16, waiting for transfers between devices: none -> 25.9 us  [the longest x1 12.1 us: body(): up = lax.ppermute(right, 'ia', y_ring(1))]
    ppermute x0 -> x16, starting transfers between devices: none -> 24.1 us  [the longest x2 3.75 us: body(): tx = [t, lax.ppermute(t, 'ja', X_LO), lax.ppermute(t, 'ia', X_HI)]]
  transfers between devices with their start and end apart: 3 -> 18, of which waited for: 3 -> 11; matrix products, arithmetic and copies ran while one was open for 10% -> 9% of each run, Pallas kernels for 0% -> 26%
where the time goes in v1:
time: 178 us
  waiting for transfers between devices  63.6 us (36%)
  Pallas kernels  49.3 us (28%)
  starting transfers between devices  36.8 us (21%)
  local copies, waits for them, and re-layouts  16.3 us (9%)
  other arithmetic  11.3 us (6%)
    all_to_all x1, waiting for transfers between devices, body(): pieces0 = lax.all_to_all(sent0, 'vert', 0, 0, tiled=True)  27.1 us
    pallas_call x2, Pallas kernels, product_near(): pl.pallas_call(near_body, out_shape=out, grid_spec=pltpu.PrefetchScalarGr...  13.5 us
    pallas_call x4, Pallas kernels, product(): pl.pallas_call(functools.partial(product_body, start), out_shape=out, gri...  13.2 us
    ppermute x1, waiting for transfers between devices, body(): up = lax.ppermute(right, 'ia', y_ring(1))  12.1 us
    all_to_all x1, waiting for transfers between devices, body(): pieces1 = lax.all_to_all(sent1_16, 'vert', 0, 0, tiled=True)  10.7 us
    pallas_call x2, Pallas kernels, turn_slabs(): pl.pallas_call(turn_body, out_shape=jax.ShapeDtypeStruct((size, count * s...  9.82 us
    unnamed x44, local copies, waits for them, and re-layouts  9.38 us
    all_to_all x1, starting transfers between devices, body(): pieces0 = lax.all_to_all(sent0, 'vert', 0, 0, tiled=True)  8.54 us
  transfers between devices with their start and end apart: 18, of which 11 were waited for; matrix products, arithmetic and copies ran while one was open for 9% of the time, Pallas kernels for 26%

profile of v1, /device:TPU:1, one launch (start us, length us, event | category | flops | bytes accessed | tf_op | source)
XLA Modules:
  0.0 177.6 jit_solution(3080859831592012050)
XLA Ops:
  0.0 2.1 %collective-permute-start.1 = (bf16[640,1280]{1,0:T(8,128)(2,1)}, bf16[640,1280]{1,0:T(8,128)(2,1)}, u32[]{:S(2)}, u32[]{:S(2)}) collective-permute-start(bf16[640,1280]{1,0:T(8,128)(2,1)} %bitcast.14), channel_id=1, source_target_pairs={{0,32},{32,64},{64,96},{96,0},{128,160},{160,192},{192,224},{224,1... | collective-permute-start | bytes 4915208 | tf_op jit(solution)/shard_map/ppermute | solution.py:315
  4.8 3.8 %shard_map.64 = bf16[640,1280]{1,0:T(8,128)(2,1)} custom-call(s32[2]{0:T(128)} %slice_add_fusion.index, bf16[10,64,5120]{2,1,0:T(8,128)(2,1)} %u.2), custom_call_target="tpu_custom_call" | custom-call | flops 1000000000 | bytes 3000000 | tf_op jit(solution)/shard_map/pallas_call | solution.py:42
  8.6 2.5 %collective-permute-start = (bf16[640,1280]{1,0:T(8,128)(2,1)}, bf16[640,1280]{1,0:T(8,128)(2,1)}, u32[]{:S(2)}, u32[]{:S(2)}) collective-permute-start(bf16[640,1280]{1,0:T(8,128)(2,1)} %shard_map.64), channel_id=1, source_target_pairs={{0,144},{8,152},{16,128},{24,136},{32,176},{40,184},{48,160},{56,1... | collective-permute-start | bytes 4915208 | tf_op jit(solution)/shard_map/ppermute | solution.py:321
  11.1 6.0 %shard_map.65.near.far = bf16[640,2560]{1,0:T(8,128)(2,1)} custom-call(s32[4]{0:T(128)} %get-tuple-element.88.index, bf16[10,64,5120]{2,1,0:T(8,128)(2,1)} %u.2), custom_call_target="tpu_custom_call" | custom-call | flops 2000000000 | bytes 6000000 | tf_op jit(solution)/shard_map/pallas_call | solution.py:42
  19.2 4.5 %shard_map.66.w = bf16[200,6400]{1,0:T(8,128)(2,1)S(1)} custom-call(bf16[10,20,6400]{2,1,0:T(8,128)(2,1)S(1)} %copy-done.11, bf16[640,640]{1,0:T(8,128)(2,1)S(1)} %fusion.1.order), custom_call_target="tpu_custom_call" | custom-call | flops 1000000000 | bytes 3000000 | tf_op jit(solution)/shard_map/pallas_call | solution.py:173
  25.2 12.1 %collective-permute-done.1.v3 = bf16[640,1280]{1,0:T(8,128)(2,1)} collective-permute-done((bf16[640,1280]{1,0:T(8,128)(2,1)}, bf16[640,1280]{1,0:T(8,128)(2,1)}, u32[]{:S(2)}, u32[]{:S(2)}) %collective-permute-start.1) | collective-permute-done | bytes 1638432 | tf_op jit(solution)/shard_map/ppermute | solution.py:315
  38.6 6.4 %shard_map.67.partial_sum = f32[640,1280]{1,0:T(8,128)S(1)} custom-call(s32[1]{0:T(128)} %constant.127.clone.1.place, bf16[640,2560]{1,0:T(8,128)(2,1)S(1)} %copy-done, bf16[640,2560]{1,0:T(8,128)(2,1)S(1)} %copy-done, bf16[640,1280]{1,0:T(8,128)(2,1)S(1)} %bitcast.16, bf16[640,1280]{1,0:T(8,128)(2,1)} %collective-permute-done.2.v1, ...), custom_call_target="tpu_custom_call" | custom-call | flops 1000000000 | bytes 3000000 | tf_op jit(solution)/shard_map/pallas_call | solution.py:82
  57.9 2.5 %collective-permute-start.5 = (bf16[200,512]{1,0:T(8,128)(2,1)S(1)}, bf16[200,512]{1,0:T(8,128)(2,1)S(1)}, u32[]{:S(2)}, u32[]{:S(2)}) collective-permute-start(bf16[200,512]{1,0:T(8,128)(2,1)S(1)} %reshape.71), channel_id=1, source_target_pairs={{0,128},{32,160},{64,192},{96,224},{128,0},{160,32},{192,64},{224,... | collective-permute-start | bytes 614408 | tf_op jit(solution)/shard_map/ppermute | solution.py:318
  62.0 7.2 %shard_map.68.partial_sum = f32[640,1280]{1,0:T(8,128)S(1)} custom-call(s32[1]{0:T(128)} %bitcast.1.place, bf16[640,1280]{1,0:T(8,128)(2,1)} %collective-permute-done.near, bf16[640,1280]{1,0:T(8,128)(2,1)} %collective-permute-done.3.far, bf16[640,1280]{1,0:T(8,128)(2,1)S(1)} %bitcast.17, bf16[640,1280]{1,0:T(8,128)(2,1)} %collective-permute-done.2.v1, ...), custom_call_target="tpu_custom_call" | custom-call | flops 1000000000 | bytes 3000000 | tf_op jit(solution)/shard_map/pallas_call | solution.py:82
  69.4 2.6 %collective-permute-done.6 = bf16[200,512]{1,0:T(8,128)(2,1)S(1)} collective-permute-done((bf16[200,512]{1,0:T(8,128)(2,1)S(1)}, bf16[200,512]{1,0:T(8,128)(2,1)S(1)}, u32[]{:S(2)}, u32[]{:S(2)}) %collective-permute-start.6) | collective-permute-done | bytes 204832 | tf_op jit(solution)/shard_map/ppermute | solution.py:319
  74.3 3.6 %shard_map.69 = f32[8,80,640]{2,1,0:T(8,128)S(1)} custom-call(s32[1]{0:T(128)} %bitcast.1.place, f32[640,1280]{1,0:T(8,128)S(1)} %shard_map.68.partial_sum, bf16[640,1280]{1,0:T(8,128)(2,1)} %collective-permute-done.near, bf16[640,1280]{1,0:T(8,128)(2,1)} %collective-permute-done.3.far, bf16[320,1280]{1,0:T(8,128)(2,1)} %collective-permute-done.7.v2a, ...), custom_call_target="tpu_custom_call" | custom-call | flops 1000000000 | bytes 3000000 | tf_op jit(solution)/shard_map/pallas_call | solution.py:129
  77.9 3.1 %shard_map.70 = f32[8,80,640]{2,1,0:T(8,128)S(1)} custom-call(s32[1]{0:T(128)} %constant.127.clone.1.place, f32[640,1280]{1,0:T(8,128)S(1)} %copy-done.2, bf16[640,2560]{1,0:T(8,128)(2,1)S(1)} %copy-done, bf16[640,2560]{1,0:T(8,128)(2,1)S(1)} %copy-done, bf16[320,1280]{1,0:T(8,128)(2,1)} %collective-permute-done.7.v2a, ...), custom_call_target="tpu_custom_call" | custom-call | flops 1000000000 | bytes 3000000 | tf_op jit(solution)/shard_map/pallas_call | solution.py:129
  82.6 3.1 %shard_map.71 = f32[8,80,640]{2,1,0:T(8,128)S(1)} custom-call(s32[1]{0:T(128)} %constant.127.clone.1.place, f32[640,1280]{1,0:T(8,128)S(1)} %copy-done.2, bf16[640,2560]{1,0:T(8,128)(2,1)S(1)} %copy-done, bf16[640,2560]{1,0:T(8,128)(2,1)S(1)} %copy-done, bf16[320,1280]{1,0:T(8,128)(2,1)} %collective-permute-done.7.v2a, ...), custom_call_target="tpu_custom_call" | custom-call | flops 1000000000 | bytes 3000000 | tf_op jit(solution)/shard_map/pallas_call | solution.py:129
  86.9 3.4 %shard_map.72 = f32[8,80,640]{2,1,0:T(8,128)S(1)} custom-call(s32[1]{0:T(128)} %bitcast.1.place, f32[640,1280]{1,0:T(8,128)S(1)} %shard_map.68.partial_sum, bf16[640,1280]{1,0:T(8,128)(2,1)} %collective-permute-done.near, bf16[640,1280]{1,0:T(8,128)(2,1)} %collective-permute-done.3.far, bf16[320,1280]{1,0:T(8,128)(2,1)} %collective-permute-done.7.v2a, ...), custom_call_target="tpu_custom_call" | custom-call | flops 1000000000 | bytes 3000000 | tf_op jit(solution)/shard_map/pallas_call | solution.py:129
  90.5 2.3 %collective-permute-done.9.up = bf16[4,200,512]{2,1,0:T(8,128)(2,1)S(1)} collective-permute-done((bf16[4,200,512]{2,1,0:T(8,128)(2,1)S(1)}, bf16[4,200,512]{2,1,0:T(8,128)(2,1)S(1)}, u32[]{:S(2)}, u32[]{:S(2)}) %collective-permute-start.9) | collective-permute-done | bytes 819232 | tf_op jit(solution)/shard_map/ppermute | solution.py:338
  93.7 2.4 %collective-permute-start.11 = (f16[8,80,640]{2,1,0:T(8,128)(2,1)S(1)}, f16[8,80,640]{2,1,0:T(8,128)(2,1)S(1)}, u32[]{:S(2)}, u32[]{:S(2)}) collective-permute-start(f16[8,80,640]{2,1,0:T(8,128)(2,1)S(1)} %multiply_convert_fusion), channel_id=1, source_target_pairs={{0,128},{32,160},{64,192},{96,224},{128,0},{160,32},{192,64},{224,... | collective-permute-start | bytes 2457608 | tf_op jit(solution)/shard_map/ppermute | solution.py:355
  96.1 8.5 %all-to-all-start.1 = ((f16[8,160,640]{2,1,0:T(8,128)(2,1)}), f16[8,160,640]{2,1,0:T(8,128)(2,1)}, u32[]{:S(2)}, u32[]{:S(2)}) async-start(f16[8,160,640]{2,1,0:T(8,128)(2,1)} %fusion), calls=%async_computation.1 | async-start | bytes 3276800 | tf_op jit(solution)/shard_map/all_to_all | solution.py:347
  107.6 4.9 %collective-permute-done.11 = f16[8,80,640]{2,1,0:T(8,128)(2,1)S(1)} collective-permute-done((f16[8,80,640]{2,1,0:T(8,128)(2,1)S(1)}, f16[8,80,640]{2,1,0:T(8,128)(2,1)S(1)}, u32[]{:S(2)}, u32[]{:S(2)}) %collective-permute-start.11) | collective-permute-done | bytes 819232 | tf_op jit(solution)/shard_map/ppermute | solution.py:355
  115.7 2.6 %collective-permute-start.14 = (bf16[4,800,512]{2,1,0:T(8,128)(2,1)S(1)}, bf16[4,800,512]{2,1,0:T(8,128)(2,1)}, u32[]{:S(2)}, u32[]{:S(2)}) collective-permute-start(bf16[4,800,512]{2,1,0:T(8,128)(2,1)S(1)} %bitcast.12), channel_id=1, source_target_pairs={{0,8},{8,0},{16,24},{24,16},{1,9},{9,1},{17,25},{25,17},{2,10},{10... | collective-permute-start | bytes 9830408 | tf_op jit(solution)/shard_map/ppermute | solution.py:366
  118.2 27.1 %all-to-all-done.1 = f16[8,160,640]{2,1,0:T(8,128)(2,1)} async-done(((f16[8,160,640]{2,1,0:T(8,128)(2,1)}), f16[8,160,640]{2,1,0:T(8,128)(2,1)}, u32[]{:S(2)}, u32[]{:S(2)}) %all-to-all-start.1) | async-done | bytes 1638432 | tf_op jit(solution)/shard_map/all_to_all | solution.py:347
  145.3 4.2 %all-to-all-start = ((f16[8,80,640]{2,1,0:T(8,128)(2,1)}), f16[8,80,640]{2,1,0:T(8,128)(2,1)}, u32[]{:S(2)}, u32[]{:S(2)}) async-start(f16[8,80,640]{2,1,0:T(8,128)(2,1)} %get-tuple-element.83), calls=%async_computation | async-start | bytes 1638400 | tf_op jit(solution)/shard_map/all_to_all | solution.py:362
  155.5 5.0 %shard_map.74.ladder = f32[10,20,512]{2,1,0:T(8,128)S(1)} custom-call(s32[3]{0:T(128)S(1)} %pad_add_fusion.1.place, bf16[200,6400]{1,0:T(8,128)(2,1)S(1)} %copy-done.4, bf16[4,800,512]{2,1,0:T(8,128)(2,1)S(1)} %bitcast.13, bf16[4,800,512]{2,1,0:T(8,128)(2,1)} %collective-permute-done.14.far), custom_call_target="tpu_custom_call" | custom-call | flops 1000000000 | bytes 3000000 | tf_op jit(solution)/shard_map/pallas_call | solution.py:249
  162.0 10.7 %all-to-all-done = f16[8,80,640]{2,1,0:T(8,128)(2,1)} async-done(((f16[8,80,640]{2,1,0:T(8,128)(2,1)}), f16[8,80,640]{2,1,0:T(8,128)(2,1)}, u32[]{:S(2)}, u32[]{:S(2)}) %all-to-all-start) | async-done | bytes 819232 | tf_op jit(solution)/shard_map/all_to_all | solution.py:362
  174.6 3.1 %shard_map.75 = bf16[10,20,512]{2,1,0:T(8,128)(2,1)} custom-call(s32[10]{0:T(128)} %dynamic_slice.26.sym_i, f32[80,640]{1,0:T(8,128)} %get-tuple-element.85.sum0, f32[80,640]{1,0:T(8,128)} %copy-done.20, f32[80,640]{1,0:T(8,128)} %convert_reduce_fusion.1.sum1, f32[80,640]{1,0:T(8,128)} %subtract_bitcast_fusion.own1, f32[10,20,512]{2,1,0:T(8,128)} %copy-done.18, ...), custom_call_target="tpu_custom_call" | custom-call | flops 1000000000 | bytes 3000000 | tf_op jit(solution)/shard_map/pallas_call | solution.py:288
  (94 shorter events, 43.8 us)
Async XLA Ops:
  0.0 37.4 %collective-permute-start.1 = (bf16[640,1280]{1,0:T(8,128)(2,1)}, bf16[640,1280]{1,0:T(8,128)(2,1)}, u32[]{:S(2)}, u32[]{:S(2)}) collective-permute-start(bf16[640,1280]{1,0:T(8,128)(2,1)} %bitcast.14), channel_id=1, source_target_pairs={{0,32},{32,64},{64,96},{96,0},{128,160},{160,192},{192,224},{224,1... | collective-permute-start | bytes 4915208 | tf_op jit(solution)/shard_map/ppermute | solution.py:315
  2.1 36.5 %collective-permute-start.2 = (bf16[640,1280]{1,0:T(8,128)(2,1)}, bf16[640,1280]{1,0:T(8,128)(2,1)}, u32[]{:S(2)}, u32[]{:S(2)}) collective-permute-start(bf16[640,1280]{1,0:T(8,128)(2,1)} %bitcast.15), channel_id=1, source_target_pairs={{0,96},{32,0},{64,32},{96,64},{128,224},{160,128},{192,160},{224,1... | collective-permute-start | bytes 4915208 | tf_op jit(solution)/shard_map/ppermute | solution.py:316
  8.6 38.1 %collective-permute-start = (bf16[640,1280]{1,0:T(8,128)(2,1)}, bf16[640,1280]{1,0:T(8,128)(2,1)}, u32[]{:S(2)}, u32[]{:S(2)}) collective-permute-start(bf16[640,1280]{1,0:T(8,128)(2,1)} %shard_map.64), channel_id=1, source_target_pairs={{0,144},{8,152},{16,128},{24,136},{32,176},{40,184},{48,160},{56,1... | collective-permute-start | bytes 4915208 | tf_op jit(solution)/shard_map/ppermute | solution.py:321
  19.2 19.4 %copy-start = (bf16[640,2560]{1,0:T(8,128)(2,1)S(1)}, bf16[640,2560]{1,0:T(8,128)(2,1)}, u32[]{:S(2)}) copy-start(bf16[640,2560]{1,0:T(8,128)(2,1)} %shard_map.65.near.far) | copy-start | bytes 9830404
  19.2 19.4 %copy-start.7 = (bf16[10,64,1280]{2,1,0:T(8,128)(2,1)S(1)}, bf16[10,64,1280]{2,1,0:T(8,128)(2,1)}, u32[]{:S(2)}) copy-start(bf16[10,64,1280]{2,1,0:T(8,128)(2,1)} %param.9) | copy-start | bytes 4915204
  46.7 13.7 %collective-permute-start.3 = (bf16[640,1280]{1,0:T(8,128)(2,1)}, bf16[640,1280]{1,0:T(8,128)(2,1)}, u32[]{:S(2)}, u32[]{:S(2)}) collective-permute-start(bf16[640,1280]{1,0:T(8,128)(2,1)} %collective-permute-done.near), channel_id=1, source_target_pairs={{0,8},{8,0},{16,24},{24,16},{1,9},{9,1},{17,25},{25,17},{2,10},{10... | collective-permute-start | bytes 4915208 | tf_op jit(solution)/shard_map/ppermute | solution.py:333
  52.9 21.4 %collective-permute-start.7 = (bf16[320,1280]{1,0:T(8,128)(2,1)}, bf16[320,1280]{1,0:T(8,128)(2,1)}, u32[]{:S(2)}, u32[]{:S(2)}) collective-permute-start(bf16[320,1280]{1,0:T(8,128)(2,1)} %slice.22), channel_id=1, source_target_pairs={{0,32},{32,64},{64,96},{96,0},{128,160},{160,192},{192,224},{224,1... | collective-permute-start | bytes 2457608 | tf_op jit(solution)/shard_map/ppermute | solution.py:328
  54.2 20.1 %collective-permute-start.8 = (bf16[320,1280]{1,0:T(8,128)(2,1)}, bf16[320,1280]{1,0:T(8,128)(2,1)}, u32[]{:S(2)}, u32[]{:S(2)}) collective-permute-start(bf16[320,1280]{1,0:T(8,128)(2,1)} %slice.23), channel_id=1, source_target_pairs={{0,96},{32,0},{64,32},{96,64},{128,224},{160,128},{192,160},{224,1... | collective-permute-start | bytes 2457608 | tf_op jit(solution)/shard_map/ppermute | solution.py:329
  56.6 12.5 %collective-permute-start.4 = (bf16[200,512]{1,0:T(8,128)(2,1)S(1)}, bf16[200,512]{1,0:T(8,128)(2,1)S(1)}, u32[]{:S(2)}, u32[]{:S(2)}) collective-permute-start(bf16[200,512]{1,0:T(8,128)(2,1)S(1)} %reshape.71), channel_id=1, source_target_pairs={{0,16},{8,24},{16,0},{24,8},{1,17},{9,25},{17,1},{25,9},{2,18},{10... | collective-permute-start | bytes 614408 | tf_op jit(solution)/shard_map/ppermute | solution.py:318
  57.9 11.5 %collective-permute-start.5 = (bf16[200,512]{1,0:T(8,128)(2,1)S(1)}, bf16[200,512]{1,0:T(8,128)(2,1)S(1)}, u32[]{:S(2)}, u32[]{:S(2)}) collective-permute-start(bf16[200,512]{1,0:T(8,128)(2,1)S(1)} %reshape.71), channel_id=1, source_target_pairs={{0,128},{32,160},{64,192},{96,224},{128,0},{160,32},{192,64},{224,... | collective-permute-start | bytes 614408 | tf_op jit(solution)/shard_map/ppermute | solution.py:318
  60.4 11.6 %collective-permute-start.6 = (bf16[200,512]{1,0:T(8,128)(2,1)S(1)}, bf16[200,512]{1,0:T(8,128)(2,1)S(1)}, u32[]{:S(2)}, u32[]{:S(2)}) collective-permute-start(bf16[200,512]{1,0:T(8,128)(2,1)S(1)} %reshape.71), channel_id=1, source_target_pairs={{0,144},{8,152},{16,128},{24,136},{32,176},{40,184},{48,160},{56,1... | collective-permute-start | bytes 614408 | tf_op jit(solution)/shard_map/ppermute | solution.py:319
  72.1 18.4 %collective-permute-start.10 = (bf16[4,200,512]{2,1,0:T(8,128)(2,1)S(1)}, bf16[4,200,512]{2,1,0:T(8,128)(2,1)S(1)}, u32[]{:S(2)}, u32[]{:S(2)}) collective-permute-start(bf16[4,200,512]{2,1,0:T(8,128)(2,1)S(1)} %pad_maximum_fusion.own), channel_id=1, source_target_pairs={{0,96},{32,0},{64,32},{96,64},{128,224},{160,128},{192,160},{224,1... | collective-permute-start | bytes 2457608 | tf_op jit(solution)/shard_map/ppermute | solution.py:339
  73.6 19.2 %collective-permute-start.9 = (bf16[4,200,512]{2,1,0:T(8,128)(2,1)S(1)}, bf16[4,200,512]{2,1,0:T(8,128)(2,1)S(1)}, u32[]{:S(2)}, u32[]{:S(2)}) collective-permute-start(bf16[4,200,512]{2,1,0:T(8,128)(2,1)S(1)} %pad_maximum_fusion.own), channel_id=1, source_target_pairs={{0,32},{32,64},{64,96},{96,0},{128,160},{160,192},{192,224},{224,1... | collective-permute-start | bytes 2457608 | tf_op jit(solution)/shard_map/ppermute | solution.py:338
  93.7 18.9 %collective-permute-start.11 = (f16[8,80,640]{2,1,0:T(8,128)(2,1)S(1)}, f16[8,80,640]{2,1,0:T(8,128)(2,1)S(1)}, u32[]{:S(2)}, u32[]{:S(2)}) collective-permute-start(f16[8,80,640]{2,1,0:T(8,128)(2,1)S(1)} %multiply_convert_fusion), channel_id=1, source_target_pairs={{0,128},{32,160},{64,192},{96,224},{128,0},{160,32},{192,64},{224,... | collective-permute-start | bytes 2457608 | tf_op jit(solution)/shard_map/ppermute | solution.py:355
  96.1 9.7 %copy-start.13 = (bf16[4,200,512]{2,1,0:T(8,128)(2,1)S(1)}, bf16[4,200,512]{2,1,0:T(8,128)(2,1)}, u32[]{:S(2)}) copy-start(bf16[4,200,512]{2,1,0:T(8,128)(2,1)} %copy-done.12) | copy-start | bytes 2457604
  96.1 49.2 %all-to-all-start.1 = ((f16[8,160,640]{2,1,0:T(8,128)(2,1)}), f16[8,160,640]{2,1,0:T(8,128)(2,1)}, u32[]{:S(2)}, u32[]{:S(2)}) async-start(f16[8,160,640]{2,1,0:T(8,128)(2,1)} %fusion), calls=%async_computation.1 | async-start | bytes 3276800 | tf_op jit(solution)/shard_map/all_to_all | solution.py:347
  104.7 10.7 %collective-permute-start.12 = (bf16[2,200,512]{2,1,0:T(8,128)(2,1)S(1)}, bf16[2,200,512]{2,1,0:T(8,128)(2,1)S(1)}, u32[]{:S(2)}, u32[]{:S(2)}) collective-permute-start(bf16[2,200,512]{2,1,0:T(8,128)(2,1)S(1)} %slice.24), channel_id=1, source_target_pairs={{0,32},{32,64},{64,96},{96,0},{128,160},{160,192},{192,224},{224,1... | collective-permute-start | bytes 1228808 | tf_op jit(solution)/shard_map/ppermute | solution.py:356
  105.8 9.5 %collective-permute-start.13 = (bf16[2,200,512]{2,1,0:T(8,128)(2,1)S(1)}, bf16[2,200,512]{2,1,0:T(8,128)(2,1)S(1)}, u32[]{:S(2)}, u32[]{:S(2)}) collective-permute-start(bf16[2,200,512]{2,1,0:T(8,128)(2,1)S(1)} %slice.25), channel_id=1, source_target_pairs={{0,96},{32,0},{64,32},{96,64},{128,224},{160,128},{192,160},{224,1... | collective-permute-start | bytes 1228808 | tf_op jit(solution)/shard_map/ppermute | solution.py:357
  115.6 33.9 %copy-start.19 = (s32[64]{0:T(128)S(1)}, s32[64]{0:T(128)}, u32[]{:S(2)}) copy-start(s32[64]{0:T(128)} %param.11) | copy-start | bytes 772
  115.6 34.1 %copy-start.21 = (s32[80]{0:T(128)S(1)}, s32[80]{0:T(128)}, u32[]{:S(2)}) copy-start(s32[80]{0:T(128)} %param.10) | copy-start | bytes 964
  115.7 39.9 %collective-permute-start.14 = (bf16[4,800,512]{2,1,0:T(8,128)(2,1)S(1)}, bf16[4,800,512]{2,1,0:T(8,128)(2,1)}, u32[]{:S(2)}, u32[]{:S(2)}) collective-permute-start(bf16[4,800,512]{2,1,0:T(8,128)(2,1)S(1)} %bitcast.12), channel_id=1, source_target_pairs={{0,8},{8,0},{16,24},{24,16},{1,9},{9,1},{17,25},{25,17},{2,10},{10... | collective-permute-start | bytes 9830408 | tf_op jit(solution)/shard_map/ppermute | solution.py:366
  145.3 27.3 %all-to-all-start = ((f16[8,80,640]{2,1,0:T(8,128)(2,1)}), f16[8,80,640]{2,1,0:T(8,128)(2,1)}, u32[]{:S(2)}, u32[]{:S(2)}) async-start(f16[8,80,640]{2,1,0:T(8,128)(2,1)} %get-tuple-element.83), calls=%async_computation | async-start | bytes 1638400 | tf_op jit(solution)/shard_map/all_to_all | solution.py:362
  155.4 6.5 %collective-permute-start.15 = (f32[80,640]{1,0:T(8,128)S(1)}, f32[80,640]{1,0:T(8,128)S(1)}, u32[]{:S(2)}, u32[]{:S(2)}) collective-permute-start(f32[80,640]{1,0:T(8,128)S(1)} %get-tuple-element.86), channel_id=1, source_target_pairs={{0,128},{32,160},{64,192},{96,224},{128,0},{160,32},{192,64},{224,... | collective-permute-start | bytes 614408 | tf_op jit(solution)/shard_map/ppermute | solution.py:372
  162.0 12.6 %copy-start.20 = (f32[80,640]{1,0:T(8,128)}, f32[80,640]{1,0:T(8,128)S(1)}, u32[]{:S(2)}) copy-start(f32[80,640]{1,0:T(8,128)S(1)} %collective-permute-done.15.own0) | copy-start | bytes 614404
  (16 other events, 70.6 us)

commit v2 on v1

--- a/solution.py
+++ b/solution.py
@@ -10,7 +10,7 @@
 F32 = jnp.float32
 BF16 = jnp.bfloat16
 SCALE = 32.0
-FIRST = 10
+FIRST = 6
 
 
 def cost(us):
@@ -261,14 +261,16 @@
     )(place.astype(jnp.int32), weights, near, far)
 
 
-def finish_body(sym_i, sum0, own0, sum1, own1, ladder, table, out, rows):
+def finish_body(sym_i, sum0, other0, sum1, ladder, table, out, rows):
     low = lax.broadcasted_iota(jnp.int32, (8, 128), 1) < 64
     for i in range(out.shape[0]):
         j = 0
-        for part, own in ((sum0, own0), (sum1, own1)):
+        for part in (sum0, sum1):
             for jp in range(part.shape[1] // 128):
                 at = slice(8 * i, 8 * i + 8), slice(128 * jp, 128 * jp + 128)
-                tile = (part[at] + own[at]) * (1.0 / SCALE)
+                tile = part[at] * (1.0 / SCALE)
+                if part is sum0:
+                    tile += other0[at] * (1.0 / SCALE)
                 turned = pltpu.roll(tile, 64, 1)
                 even = jnp.where(low, tile, pltpu.roll(turned, 7, 0))
                 odd = jnp.where(low, turned, pltpu.roll(tile, 7, 0))
@@ -355,17 +357,14 @@
     theirs1 = lax.ppermute(theirs1, "ia", X_HI)
     t_two_a = lax.ppermute(t_up[:2], "ia", y_ring(1))
     t_two_b = lax.ppermute(t_down[2:], "ia", y_ring(-1))
-    sent1 = ours1 * SCALE + theirs1.astype(F32)
-    sent1_16 = sent1.astype(jnp.float16)
-    own1 = lax.dynamic_index_in_dim(sent1, z, 0, keepdims=False)
-    own1 -= lax.dynamic_index_in_dim(sent1_16, z, 0, keepdims=False).astype(F32)
+    sent1_16 = (ours1 * SCALE + theirs1.astype(F32)).astype(jnp.float16)
     pieces1 = lax.all_to_all(sent1_16, "vert", 0, 0, tiled=True)
 
     tx, t_down, t_two_a, t_two_b, t_up, sent1_16 = after(tx, t_down, t_two_a, t_two_b, t_up, sent1_16)
     near = order_pieces(y, (tx, t_down, t_two_a, t_two_b, t_up))
     far = lax.ppermute(near, "ja", CORE)
 
-    pieces0, sent1_16, own1, near = after(pieces0, sent1_16, own1, near)
+    pieces0, sent1_16, near = after(pieces0, sent1_16, near)
     ladder = ladder_sum(jnp.stack([h, ja // 2, core]), weights, near, far, rows_i)
     sum0 = jnp.sum(pieces0.astype(F32), axis=0)
     size = sum0.shape[0] // 2
@@ -378,7 +377,7 @@
     table = jnp.bitwise_xor(sym_j[:, None], sym_ab[None, :])
     pieces1, ladder, other0, table, sym_i = after(pieces1, ladder, other0, table, sym_i)
     sum1 = jnp.sum(pieces1.astype(F32), axis=0)
-    return finish(sym_i, (sum0[:size], other0, sum1, own1), ladder, table)
+    return finish(sym_i, (sum0[:size], other0, sum1), ladder, table)
 
 
 def solution(mesh):

time: 178 us -> 174 us (0.978)
  waiting for transfers between devices: 63.6 us -> 53.6 us
  local copies, waits for them, and re-layouts: 16.3 us -> 20 us
    all_to_all x1, waiting for transfers between devices: 27.1 us -> 3.98 us  [body(): pieces0 = lax.all_to_all(sent0, 'vert', 0, 0, tiled=True)]
    all_to_all x1, waiting for transfers between devices: 10.7 us -> 18.6 us  [body(): pieces1 = lax.all_to_all(sent1_16, 'vert', 0, 0, tiled=True)]
    ppermute x1, waiting for transfers between devices: 4.94 us -> 12.3 us  [body(): theirs1 = lax.ppermute(theirs1, 'ia', X_HI)]
    unnamed x44 -> x48, local copies, waits for them, and re-layouts: 9.38 us -> 12.5 us
    sub x1 -> x0, other arithmetic: 1.85 us -> none  [body(): own1 -= lax.dynamic_index_in_dim(sent1_16, z, 0, keepdims=False).astype(F32)]
  transfers between devices with their start and end apart: 18 -> 18, of which waited for: 11 -> 9; matrix products, arithmetic and copies ran while one was open for 9% -> 9% of each run, Pallas kernels for 26% -> 27%
where the time goes in v2:
time: 174 us; the launch traced here: 173 us
  waiting for transfers between devices  53.6 us (31%)
  Pallas kernels  49.9 us (29%)
  starting transfers between devices  38.5 us (22%)
  local copies, waits for them, and re-layouts  20 us (11%)
  other arithmetic  11 us (6%)
    all_to_all x1, waiting for transfers between devices, body(): pieces1 = lax.all_to_all(sent1_16, 'vert', 0, 0, tiled=True)  18.6 us
    pallas_call x4, Pallas kernels, product(): pl.pallas_call(functools.partial(product_body, start), out_shape=out, gri...  13.9 us
    pallas_call x2, Pallas kernels, product_near(): pl.pallas_call(near_body, out_shape=out, grid_spec=pltpu.PrefetchScalarGr...  13.5 us
    unnamed x48, local copies, waits for them, and re-layouts  12.5 us
    ppermute x1, waiting for transfers between devices, body(): theirs1 = lax.ppermute(theirs1, 'ia', X_HI)  12.3 us
    ppermute x1, waiting for transfers between devices, body(): up = lax.ppermute(right, 'ia', y_ring(1))  12 us
    pallas_call x2, Pallas kernels, turn_slabs(): pl.pallas_call(turn_body, out_shape=jax.ShapeDtypeStruct((size, count * s...  9.89 us
    all_to_all x1, starting transfers between devices, body(): pieces0 = lax.all_to_all(sent0, 'vert', 0, 0, tiled=True)  8.19 us
  transfers between devices with their start and end apart: 18, of which 9 were waited for; matrix products, arithmetic and copies ran while one was open for 9% of the time, Pallas kernels for 27%

profile of v2, /device:TPU:1, one launch (start us, length us, event | category | flops | bytes accessed | tf_op | source)
XLA Modules:
  0.0 173.3 jit_solution(5043844214615531215)
XLA Ops:
  0.0 2.1 %collective-permute-start.1 = (bf16[640,1280]{1,0:T(8,128)(2,1)}, bf16[640,1280]{1,0:T(8,128)(2,1)}, u32[]{:S(2)}, u32[]{:S(2)}) collective-permute-start(bf16[640,1280]{1,0:T(8,128)(2,1)} %bitcast.12), channel_id=1, source_target_pairs={{0,32},{32,64},{64,96},{96,0},{128,160},{160,192},{192,224},{224,1... | collective-permute-start | bytes 4915208 | tf_op jit(solution)/shard_map/ppermute | solution.py:317
  4.8 3.8 %shard_map.64 = bf16[640,1280]{1,0:T(8,128)(2,1)} custom-call(s32[2]{0:T(128)} %slice_add_fusion.index, bf16[10,64,5120]{2,1,0:T(8,128)(2,1)} %u.2), custom_call_target="tpu_custom_call" | custom-call | flops 1000000000 | bytes 3000000 | tf_op jit(solution)/shard_map/pallas_call | solution.py:42
  8.7 2.5 %collective-permute-start = (bf16[640,1280]{1,0:T(8,128)(2,1)}, bf16[640,1280]{1,0:T(8,128)(2,1)}, u32[]{:S(2)}, u32[]{:S(2)}) collective-permute-start(bf16[640,1280]{1,0:T(8,128)(2,1)} %shard_map.64), channel_id=1, source_target_pairs={{0,144},{8,152},{16,128},{24,136},{32,176},{40,184},{48,160},{56,1... | collective-permute-start | bytes 4915208 | tf_op jit(solution)/shard_map/ppermute | solution.py:323
  11.2 6.0 %shard_map.65.near.far = bf16[640,2560]{1,0:T(8,128)(2,1)} custom-call(s32[4]{0:T(128)} %get-tuple-element.84.index, bf16[10,64,5120]{2,1,0:T(8,128)(2,1)} %u.2), custom_call_target="tpu_custom_call" | custom-call | flops 2000000000 | bytes 6000000 | tf_op jit(solution)/shard_map/pallas_call | solution.py:42
  19.4 4.5 %shard_map.66.w = bf16[200,6400]{1,0:T(8,128)(2,1)S(1)} custom-call(bf16[10,20,6400]{2,1,0:T(8,128)(2,1)S(1)} %copy-done.11, bf16[640,640]{1,0:T(8,128)(2,1)S(1)} %fusion.1.order), custom_call_target="tpu_custom_call" | custom-call | flops 1000000000 | bytes 3000000 | tf_op jit(solution)/shard_map/pallas_call | solution.py:173
  25.3 12.0 %collective-permute-done.1.v3 = bf16[640,1280]{1,0:T(8,128)(2,1)} collective-permute-done((bf16[640,1280]{1,0:T(8,128)(2,1)}, bf16[640,1280]{1,0:T(8,128)(2,1)}, u32[]{:S(2)}, u32[]{:S(2)}) %collective-permute-start.1) | collective-permute-done | bytes 1638432 | tf_op jit(solution)/shard_map/ppermute | solution.py:317
  38.6 6.4 %shard_map.67.partial_sum = f32[640,1280]{1,0:T(8,128)S(1)} custom-call(s32[1]{0:T(128)} %constant.119.clone.1.place, bf16[640,2560]{1,0:T(8,128)(2,1)S(1)} %copy-done, bf16[640,2560]{1,0:T(8,128)(2,1)S(1)} %copy-done, bf16[640,1280]{1,0:T(8,128)(2,1)S(1)} %bitcast.14, bf16[640,1280]{1,0:T(8,128)(2,1)} %collective-permute-done.2.v1, ...), custom_call_target="tpu_custom_call" | custom-call | flops 1000000000 | bytes 3000000 | tf_op jit(solution)/shard_map/pallas_call | solution.py:82
  57.9 2.5 %collective-permute-start.5 = (bf16[200,512]{1,0:T(8,128)(2,1)S(1)}, bf16[200,512]{1,0:T(8,128)(2,1)S(1)}, u32[]{:S(2)}, u32[]{:S(2)}) collective-permute-start(bf16[200,512]{1,0:T(8,128)(2,1)S(1)} %reshape.69), channel_id=1, source_target_pairs={{0,128},{32,160},{64,192},{96,224},{128,0},{160,32},{192,64},{224,... | collective-permute-start | bytes 614408 | tf_op jit(solution)/shard_map/ppermute | solution.py:320
  62.0 7.2 %shard_map.68.partial_sum = f32[640,1280]{1,0:T(8,128)S(1)} custom-call(s32[1]{0:T(128)} %bitcast.1.place, bf16[640,1280]{1,0:T(8,128)(2,1)} %collective-permute-done.near, bf16[640,1280]{1,0:T(8,128)(2,1)} %collective-permute-done.3.far, bf16[640,1280]{1,0:T(8,128)(2,1)S(1)} %bitcast.15, bf16[640,1280]{1,0:T(8,128)(2,1)} %collective-permute-done.2.v1, ...), custom_call_target="tpu_custom_call" | custom-call | flops 1000000000 | bytes 3000000 | tf_op jit(solution)/shard_map/pallas_call | solution.py:82
  69.4 2.6 %collective-permute-done.6 = bf16[200,512]{1,0:T(8,128)(2,1)S(1)} collective-permute-done((bf16[200,512]{1,0:T(8,128)(2,1)S(1)}, bf16[200,512]{1,0:T(8,128)(2,1)S(1)}, u32[]{:S(2)}, u32[]{:S(2)}) %collective-permute-start.6) | collective-permute-done | bytes 204832 | tf_op jit(solution)/shard_map/ppermute | solution.py:321
  74.3 3.2 %shard_map.69 = f32[8,80,384]{2,1,0:T(8,128)S(1)} custom-call(s32[1]{0:T(128)} %bitcast.1.place, f32[640,1280]{1,0:T(8,128)S(1)} %shard_map.68.partial_sum, bf16[640,1280]{1,0:T(8,128)(2,1)} %collective-permute-done.near, bf16[640,1280]{1,0:T(8,128)(2,1)} %collective-permute-done.3.far, bf16[320,1280]{1,0:T(8,128)(2,1)} %collective-permute-done.7.v2a, ...), custom_call_target="tpu_custom_call" | custom-call | flops 1000000000 | bytes 3000000 | tf_op jit(solution)/shard_map/pallas_call | solution.py:129
  77.6 2.7 %shard_map.70 = f32[8,80,384]{2,1,0:T(8,128)S(1)} custom-call(s32[1]{0:T(128)} %constant.119.clone.1.place, f32[640,1280]{1,0:T(8,128)S(1)} %copy-done.2, bf16[640,2560]{1,0:T(8,128)(2,1)S(1)} %copy-done, bf16[640,2560]{1,0:T(8,128)(2,1)S(1)} %copy-done, bf16[320,1280]{1,0:T(8,128)(2,1)} %collective-permute-done.7.v2a, ...), custom_call_target="tpu_custom_call" | custom-call | flops 1000000000 | bytes 3000000 | tf_op jit(solution)/shard_map/pallas_call | solution.py:129
  81.5 3.4 %shard_map.71 = f32[8,80,896]{2,1,0:T(8,128)S(1)} custom-call(s32[1]{0:T(128)} %constant.119.clone.1.place, f32[640,1280]{1,0:T(8,128)S(1)} %copy-done.2, bf16[640,2560]{1,0:T(8,128)(2,1)S(1)} %copy-done, bf16[640,2560]{1,0:T(8,128)(2,1)S(1)} %copy-done, bf16[320,1280]{1,0:T(8,128)(2,1)} %collective-permute-done.7.v2a, ...), custom_call_target="tpu_custom_call" | custom-call | flops 1000000000 | bytes 3000000 | tf_op jit(solution)/shard_map/pallas_call | solution.py:129
  85.0 4.6 %shard_map.72 = f32[8,80,896]{2,1,0:T(8,128)S(1)} custom-call(s32[1]{0:T(128)} %bitcast.1.place, f32[640,1280]{1,0:T(8,128)S(1)} %shard_map.68.partial_sum, bf16[640,1280]{1,0:T(8,128)(2,1)} %collective-permute-done.near, bf16[640,1280]{1,0:T(8,128)(2,1)} %collective-permute-done.3.far, bf16[320,1280]{1,0:T(8,128)(2,1)} %collective-permute-done.7.v2a, ...), custom_call_target="tpu_custom_call" | custom-call | flops 1000000000 | bytes 3000000 | tf_op jit(solution)/shard_map/pallas_call | solution.py:129
  98.2 8.2 %all-to-all-start.1 = ((f16[8,160,384]{2,1,0:T(8,128)(2,1)}), f16[8,160,384]{2,1,0:T(8,128)(2,1)}, u32[]{:S(2)}, u32[]{:S(2)}) async-start(f16[8,160,384]{2,1,0:T(8,128)(2,1)} %fusion), calls=%async_computation.1 | async-start | bytes 1966080 | tf_op jit(solution)/shard_map/all_to_all | solution.py:349
  106.4 12.3 %collective-permute-done.11 = f16[8,80,896]{2,1,0:T(8,128)(2,1)} collective-permute-done((f16[8,80,896]{2,1,0:T(8,128)(2,1)}, f16[8,80,896]{2,1,0:T(8,128)(2,1)}, u32[]{:S(2)}, u32[]{:S(2)}) %collective-permute-start.11) | collective-permute-done | bytes 1146912 | tf_op jit(solution)/shard_map/ppermute | solution.py:357
  118.6 2.6 %add_convert_fusion = f16[8,80,896]{2,1,0:T(8,128)(2,1)} fusion(f16[8,80,896]{2,1,0:T(8,128)(2,1)} %collective-permute-done.11, f32[8,80,896]{2,1,0:T(8,128)S(1)} %copy-done.6), kind=kLoop, calls=%fused_computation.1 | loop fusion | flops 2293760 | bytes 4587520 | tf_op jit(solution)/shard_map/convert_element_type | solution.py:360
  125.0 3.7 %collective-permute-start.14 = (bf16[4,800,512]{2,1,0:T(8,128)(2,1)S(1)}, bf16[4,800,512]{2,1,0:T(8,128)(2,1)}, u32[]{:S(2)}, u32[]{:S(2)}) collective-permute-start(bf16[4,800,512]{2,1,0:T(8,128)(2,1)S(1)} %bitcast.10), channel_id=1, source_target_pairs={{0,8},{8,0},{16,24},{24,16},{1,9},{9,1},{17,25},{25,17},{2,10},{10... | collective-permute-start | bytes 9830408 | tf_op jit(solution)/shard_map/ppermute | solution.py:365
  128.7 4.0 %all-to-all-done.1 = f16[8,160,384]{2,1,0:T(8,128)(2,1)} async-done(((f16[8,160,384]{2,1,0:T(8,128)(2,1)}), f16[8,160,384]{2,1,0:T(8,128)(2,1)}, u32[]{:S(2)}, u32[]{:S(2)}) %all-to-all-start.1) | async-done | bytes 983072 | tf_op jit(solution)/shard_map/all_to_all | solution.py:349
  132.7 4.2 %all-to-all-start = ((f16[8,80,896]{2,1,0:T(8,128)(2,1)}), f16[8,80,896]{2,1,0:T(8,128)(2,1)}, u32[]{:S(2)}, u32[]{:S(2)}) async-start(f16[8,80,896]{2,1,0:T(8,128)(2,1)} %add_convert_fusion), calls=%async_computation | async-start | bytes 2293760 | tf_op jit(solution)/shard_map/all_to_all | solution.py:361
  143.9 5.0 %shard_map.74.ladder = f32[10,20,512]{2,1,0:T(8,128)S(1)} custom-call(s32[3]{0:T(128)S(1)} %pad_add_fusion.1.place, bf16[200,6400]{1,0:T(8,128)(2,1)S(1)} %copy-done.4, bf16[4,800,512]{2,1,0:T(8,128)(2,1)S(1)} %bitcast.11, bf16[4,800,512]{2,1,0:T(8,128)(2,1)} %collective-permute-done.14.far), custom_call_target="tpu_custom_call" | custom-call | flops 1000000000 | bytes 3000000 | tf_op jit(solution)/shard_map/pallas_call | solution.py:249
  149.7 18.6 %all-to-all-done = f16[8,80,896]{2,1,0:T(8,128)(2,1)} async-done(((f16[8,80,896]{2,1,0:T(8,128)(2,1)}), f16[8,80,896]{2,1,0:T(8,128)(2,1)}, u32[]{:S(2)}, u32[]{:S(2)}) %all-to-all-start) | async-done | bytes 1146912 | tf_op jit(solution)/shard_map/all_to_all | solution.py:361
  168.3 2.1 %convert_reduce_fusion.sum1 = f32[80,896]{1,0:T(8,128)} fusion(f16[8,80,896]{2,1,0:T(8,128)(2,1)} %all-to-all-done), kind=kLoop, calls=%fused_computation | loop fusion | flops 1075200 | bytes 1433600 | tf_op jit(solution)/shard_map/reduce_sum | solution.py:379
  170.5 2.9 %shard_map.75 = bf16[10,20,512]{2,1,0:T(8,128)(2,1)} custom-call(s32[10]{0:T(128)} %dynamic_slice.16.sym_i, f32[80,384]{1,0:T(8,128)} %get-tuple-element.81.sum0, f32[80,384]{1,0:T(8,128)} %copy-done.22, f32[80,896]{1,0:T(8,128)} %convert_reduce_fusion.sum1, f32[10,20,512]{2,1,0:T(8,128)} %copy-done.16, s32[20,512]{1,0:T(8,128)} %broadcast_xor_fusion.table), custom_call_target="tpu_custom_call" | custom-call | flops 1000000000 | bytes 3000000 | tf_op jit(solution)/shard_map/pallas_call | solution.py:290
  (97 shorter events, 45.9 us)
Async XLA Ops:
  0.0 37.4 %collective-permute-start.1 = (bf16[640,1280]{1,0:T(8,128)(2,1)}, bf16[640,1280]{1,0:T(8,128)(2,1)}, u32[]{:S(2)}, u32[]{:S(2)}) collective-permute-start(bf16[640,1280]{1,0:T(8,128)(2,1)} %bitcast.12), channel_id=1, source_target_pairs={{0,32},{32,64},{64,96},{96,0},{128,160},{160,192},{192,224},{224,1... | collective-permute-start | bytes 4915208 | tf_op jit(solution)/shard_map/ppermute | solution.py:317
  2.1 36.5 %collective-permute-start.2 = (bf16[640,1280]{1,0:T(8,128)(2,1)}, bf16[640,1280]{1,0:T(8,128)(2,1)}, u32[]{:S(2)}, u32[]{:S(2)}) collective-permute-start(bf16[640,1280]{1,0:T(8,128)(2,1)} %bitcast.13), channel_id=1, source_target_pairs={{0,96},{32,0},{64,32},{96,64},{128,224},{160,128},{192,160},{224,1... | collective-permute-start | bytes 4915208 | tf_op jit(solution)/shard_map/ppermute | solution.py:318
  8.7 38.0 %collective-permute-start = (bf16[640,1280]{1,0:T(8,128)(2,1)}, bf16[640,1280]{1,0:T(8,128)(2,1)}, u32[]{:S(2)}, u32[]{:S(2)}) collective-permute-start(bf16[640,1280]{1,0:T(8,128)(2,1)} %shard_map.64), channel_id=1, source_target_pairs={{0,144},{8,152},{16,128},{24,136},{32,176},{40,184},{48,160},{56,1... | collective-permute-start | bytes 4915208 | tf_op jit(solution)/shard_map/ppermute | solution.py:323
  19.4 19.3 %copy-start = (bf16[640,2560]{1,0:T(8,128)(2,1)S(1)}, bf16[640,2560]{1,0:T(8,128)(2,1)}, u32[]{:S(2)}) copy-start(bf16[640,2560]{1,0:T(8,128)(2,1)} %shard_map.65.near.far) | copy-start | bytes 9830404
  19.4 19.3 %copy-start.7 = (bf16[10,64,1280]{2,1,0:T(8,128)(2,1)S(1)}, bf16[10,64,1280]{2,1,0:T(8,128)(2,1)}, u32[]{:S(2)}) copy-start(bf16[10,64,1280]{2,1,0:T(8,128)(2,1)} %param.9) | copy-start | bytes 4915204
  46.7 13.6 %collective-permute-start.3 = (bf16[640,1280]{1,0:T(8,128)(2,1)}, bf16[640,1280]{1,0:T(8,128)(2,1)}, u32[]{:S(2)}, u32[]{:S(2)}) collective-permute-start(bf16[640,1280]{1,0:T(8,128)(2,1)} %collective-permute-done.near), channel_id=1, source_target_pairs={{0,8},{8,0},{16,24},{24,16},{1,9},{9,1},{17,25},{25,17},{2,10},{10... | collective-permute-start | bytes 4915208 | tf_op jit(solution)/shard_map/ppermute | solution.py:335
  52.9 21.4 %collective-permute-start.7 = (bf16[320,1280]{1,0:T(8,128)(2,1)}, bf16[320,1280]{1,0:T(8,128)(2,1)}, u32[]{:S(2)}, u32[]{:S(2)}) collective-permute-start(bf16[320,1280]{1,0:T(8,128)(2,1)} %slice.22), channel_id=1, source_target_pairs={{0,32},{32,64},{64,96},{96,0},{128,160},{160,192},{192,224},{224,1... | collective-permute-start | bytes 2457608 | tf_op jit(solution)/shard_map/ppermute | solution.py:330
  54.2 20.1 %collective-permute-start.8 = (bf16[320,1280]{1,0:T(8,128)(2,1)}, bf16[320,1280]{1,0:T(8,128)(2,1)}, u32[]{:S(2)}, u32[]{:S(2)}) collective-permute-start(bf16[320,1280]{1,0:T(8,128)(2,1)} %slice.23), channel_id=1, source_target_pairs={{0,96},{32,0},{64,32},{96,64},{128,224},{160,128},{192,160},{224,1... | collective-permute-start | bytes 2457608 | tf_op jit(solution)/shard_map/ppermute | solution.py:331
  56.6 12.5 %collective-permute-start.4 = (bf16[200,512]{1,0:T(8,128)(2,1)S(1)}, bf16[200,512]{1,0:T(8,128)(2,1)S(1)}, u32[]{:S(2)}, u32[]{:S(2)}) collective-permute-start(bf16[200,512]{1,0:T(8,128)(2,1)S(1)} %reshape.69), channel_id=1, source_target_pairs={{0,16},{8,24},{16,0},{24,8},{1,17},{9,25},{17,1},{25,9},{2,18},{10... | collective-permute-start | bytes 614408 | tf_op jit(solution)/shard_map/ppermute | solution.py:320
  57.9 11.5 %collective-permute-start.5 = (bf16[200,512]{1,0:T(8,128)(2,1)S(1)}, bf16[200,512]{1,0:T(8,128)(2,1)S(1)}, u32[]{:S(2)}, u32[]{:S(2)}) collective-permute-start(bf16[200,512]{1,0:T(8,128)(2,1)S(1)} %reshape.69), channel_id=1, source_target_pairs={{0,128},{32,160},{64,192},{96,224},{128,0},{160,32},{192,64},{224,... | collective-permute-start | bytes 614408 | tf_op jit(solution)/shard_map/ppermute | solution.py:320
  60.3 11.6 %collective-permute-start.6 = (bf16[200,512]{1,0:T(8,128)(2,1)S(1)}, bf16[200,512]{1,0:T(8,128)(2,1)S(1)}, u32[]{:S(2)}, u32[]{:S(2)}) collective-permute-start(bf16[200,512]{1,0:T(8,128)(2,1)S(1)} %reshape.69), channel_id=1, source_target_pairs={{0,144},{8,152},{16,128},{24,136},{32,176},{40,184},{48,160},{56,1... | collective-permute-start | bytes 614408 | tf_op jit(solution)/shard_map/ppermute | solution.py:321
  72.1 18.7 %collective-permute-start.10 = (bf16[4,200,512]{2,1,0:T(8,128)(2,1)S(1)}, bf16[4,200,512]{2,1,0:T(8,128)(2,1)S(1)}, u32[]{:S(2)}, u32[]{:S(2)}) collective-permute-start(bf16[4,200,512]{2,1,0:T(8,128)(2,1)S(1)} %pad_maximum_fusion.own), channel_id=1, source_target_pairs={{0,96},{32,0},{64,32},{96,64},{128,224},{160,128},{192,160},{224,1... | collective-permute-start | bytes 2457608 | tf_op jit(solution)/shard_map/ppermute | solution.py:341
  73.6 19.2 %collective-permute-start.9 = (bf16[4,200,512]{2,1,0:T(8,128)(2,1)S(1)}, bf16[4,200,512]{2,1,0:T(8,128)(2,1)S(1)}, u32[]{:S(2)}, u32[]{:S(2)}) collective-permute-start(bf16[4,200,512]{2,1,0:T(8,128)(2,1)S(1)} %pad_maximum_fusion.own), channel_id=1, source_target_pairs={{0,32},{32,64},{64,96},{96,0},{128,160},{160,192},{192,224},{224,1... | collective-permute-start | bytes 2457608 | tf_op jit(solution)/shard_map/ppermute | solution.py:340
  90.8 27.8 %copy-start.6 = (f32[8,80,896]{2,1,0:T(8,128)S(1)}, f32[8,80,896]{2,1,0:T(8,128)}, u32[]{:S(2)}) copy-start(f32[8,80,896]{2,1,0:T(8,128)} %copy-done.5) | copy-start | bytes 6881284
  92.7 25.9 %collective-permute-start.11 = (f16[8,80,896]{2,1,0:T(8,128)(2,1)}, f16[8,80,896]{2,1,0:T(8,128)(2,1)}, u32[]{:S(2)}, u32[]{:S(2)}) collective-permute-start(f16[8,80,896]{2,1,0:T(8,128)(2,1)} %multiply_convert_fusion), channel_id=1, source_target_pairs={{0,128},{32,160},{64,192},{96,224},{128,0},{160,32},{192,64},{224,... | collective-permute-start | bytes 3440648 | tf_op jit(solution)/shard_map/ppermute | solution.py:357
  94.4 26.9 %collective-permute-start.12 = (bf16[2,200,512]{2,1,0:T(8,128)(2,1)S(1)}, bf16[2,200,512]{2,1,0:T(8,128)(2,1)S(1)}, u32[]{:S(2)}, u32[]{:S(2)}) collective-permute-start(bf16[2,200,512]{2,1,0:T(8,128)(2,1)S(1)} %slice.24), channel_id=1, source_target_pairs={{0,32},{32,64},{64,96},{96,0},{128,160},{160,192},{192,224},{224,1... | collective-permute-start | bytes 1228808 | tf_op jit(solution)/shard_map/ppermute | solution.py:358
  96.5 25.5 %collective-permute-start.13 = (bf16[2,200,512]{2,1,0:T(8,128)(2,1)}, bf16[2,200,512]{2,1,0:T(8,128)(2,1)S(1)}, u32[]{:S(2)}, u32[]{:S(2)}) collective-permute-start(bf16[2,200,512]{2,1,0:T(8,128)(2,1)} %slice.25), channel_id=1, source_target_pairs={{0,96},{32,0},{64,32},{96,64},{128,224},{160,128},{192,160},{224,1... | collective-permute-start | bytes 1228808 | tf_op jit(solution)/shard_map/ppermute | solution.py:359
  98.2 34.5 %all-to-all-start.1 = ((f16[8,160,384]{2,1,0:T(8,128)(2,1)}), f16[8,160,384]{2,1,0:T(8,128)(2,1)}, u32[]{:S(2)}, u32[]{:S(2)}) async-start(f16[8,160,384]{2,1,0:T(8,128)(2,1)} %fusion), calls=%async_computation.1 | async-start | bytes 1966080 | tf_op jit(solution)/shard_map/all_to_all | solution.py:349
  106.3 16.4 %copy-start.10 = (bf16[4,200,512]{2,1,0:T(8,128)(2,1)S(1)}, bf16[4,200,512]{2,1,0:T(8,128)(2,1)}, u32[]{:S(2)}) copy-start(bf16[4,200,512]{2,1,0:T(8,128)(2,1)} %copy-done.9) | copy-start | bytes 2457604
  106.4 16.4 %copy-start.13 = (bf16[4,200,512]{2,1,0:T(8,128)(2,1)S(1)}, bf16[4,200,512]{2,1,0:T(8,128)(2,1)}, u32[]{:S(2)}) copy-start(bf16[4,200,512]{2,1,0:T(8,128)(2,1)} %copy-done.12) | copy-start | bytes 2457604
  125.0 17.2 %collective-permute-start.14 = (bf16[4,800,512]{2,1,0:T(8,128)(2,1)S(1)}, bf16[4,800,512]{2,1,0:T(8,128)(2,1)}, u32[]{:S(2)}, u32[]{:S(2)}) collective-permute-start(bf16[4,800,512]{2,1,0:T(8,128)(2,1)S(1)} %bitcast.10), channel_id=1, source_target_pairs={{0,8},{8,0},{16,24},{24,16},{1,9},{9,1},{17,25},{25,17},{2,10},{10... | collective-permute-start | bytes 9830408 | tf_op jit(solution)/shard_map/ppermute | solution.py:365
  132.7 35.6 %all-to-all-start = ((f16[8,80,896]{2,1,0:T(8,128)(2,1)}), f16[8,80,896]{2,1,0:T(8,128)(2,1)}, u32[]{:S(2)}, u32[]{:S(2)}) async-start(f16[8,80,896]{2,1,0:T(8,128)(2,1)} %add_convert_fusion), calls=%async_computation | async-start | bytes 2293760 | tf_op jit(solution)/shard_map/all_to_all | solution.py:361
  140.0 9.7 %collective-permute-start.15 = (f32[80,384]{1,0:T(8,128)S(1)}, f32[80,384]{1,0:T(8,128)S(1)}, u32[]{:S(2)}, u32[]{:S(2)}) collective-permute-start(f32[80,384]{1,0:T(8,128)S(1)} %get-tuple-element.82), channel_id=1, source_target_pairs={{0,128},{32,160},{64,192},{96,224},{128,0},{160,32},{192,64},{224,... | collective-permute-start | bytes 368648 | tf_op jit(solution)/shard_map/ppermute | solution.py:371
  149.7 20.7 %copy-start.22 = (f32[80,384]{1,0:T(8,128)}, f32[80,384]{1,0:T(8,128)S(1)}, u32[]{:S(2)}) copy-start(f32[80,384]{1,0:T(8,128)S(1)} %collective-permute-done.15.other0) | copy-start | bytes 368644
  (18 other events, 75.1 us)

commit v3 on v2

--- a/solution.py
+++ b/solution.py
@@ -53,7 +53,8 @@
     )(index.astype(jnp.int32), u)
 
 
-def near_body(place, near, far, v0, v1, v3, out, left, right):
+def near_body(place, near, far, v0, v1, v3, *refs):
+    out, left, right = refs[-3:]
     size = near.shape[0]
 
     @pl.when(place[0] == 0)
@@ -74,7 +75,7 @@
         out[low:high, :] = total + jnp.dot(left[low:high, :], v0[...], preferred_element_type=F32)
 
 
-def product_near(place, left, parts):
+def product_near(place, left, parts, *tokens):
     size, width = parts[0].shape
     side = lambda at: pl.BlockSpec((size, 2 * size), lambda s, place: (0, at))
     whole = lambda x: pl.BlockSpec(x.shape, lambda s, place: (0,) * x.ndim)
@@ -85,13 +86,15 @@
         grid_spec=pltpu.PrefetchScalarGridSpec(
             num_scalar_prefetch=1,
             grid=(1,),
-            in_specs=[side(0), side(2 - len(left))] + [whole(x) for x in parts],
+            in_specs=[side(0), side(2 - len(left))]
+            + [whole(x) for x in parts]
+            + [pl.BlockSpec(memory_space=pl.ANY)] * len(tokens),
             out_specs=whole(out),
             scratch_shapes=[pltpu.VMEM((size, size), BF16), pltpu.VMEM((2 * size, width), BF16)],
         ),
         compiler_params=pltpu.CompilerParams(vmem_limit_bytes=32 << 20),
         cost_estimate=cost(1),
-    )(place.astype(jnp.int32).reshape(1), left[0], left[-1], *parts)
+    )(place.astype(jnp.int32).reshape(1), left[0], left[-1], *parts, *tokens)
 
 
 def product_body(start, place, partial_sum, near, far, v2a, v2b, out, left):
@@ -330,7 +333,7 @@
     v2a = lax.ppermute(up[:half], "ia", y_ring(1))
     v2b = lax.ppermute(down[half:], "ia", y_ring(-1))
     flat = jnp.zeros_like(z)
-    ours = product_near(flat, (left,), (right, down, up))
+    ours = product_near(flat, (left,), (right, down, up), tx[1])
     got, ours = after(got, ours)
     got_core = lax.ppermute(got, "ja", CORE)
     theirs = product_near(core, (got, got_core), (right, down, up))

time: 174 us -> 171 us (0.983)
  Pallas kernels: 49.9 us -> 40.8 us
  waiting for transfers between devices: 53.6 us -> 62.5 us
  starting transfers between devices: 38.5 us -> 35.7 us
  local copies, waits for them, and re-layouts: 20 us -> 17.5 us
    pallas_call x4, Pallas kernels: 13.9 us -> 6.7 us  [product(): pl.pallas_call(functools.partial(product_body, start), out_shape=out, gri...]
    ppermute x1, waiting for transfers between devices: 0.01 us -> 5.92 us  [body(): t_down = lax.ppermute(tx, 'ia', y_ring(-1))]
    ppermute x1, waiting for transfers between devices: 12 us -> 8.74 us  [body(): up = lax.ppermute(right, 'ia', y_ring(1))]
    ppermute x1, waiting for transfers between devices: 0.72 us -> 3.85 us  [body(): v2a = lax.ppermute(up[:half], 'ia', y_ring(1))]
    ppermute x1, waiting for transfers between devices: 2.56 us -> 4.71 us  [body(): tx.append(lax.ppermute(t, ('ia', 'ja'), X_CROSS))]
    all_to_all x1, waiting for transfers between devices: 18.6 us -> 16.5 us  [body(): pieces1 = lax.all_to_all(sent1_16, 'vert', 0, 0, tiled=True)]
    ppermute x2, starting transfers between devices: 3.75 us -> 1.63 us  [body(): tx = [t, lax.ppermute(t, 'ja', X_LO), lax.ppermute(t, 'ia', X_HI)]]
    slice x1, local copies, waits for them, and re-layouts: 2.09 us -> 0.05 us  [body(): v2a = lax.ppermute(up[:half], 'ia', y_ring(1))]
  transfers between devices with their start and end apart: 18 -> 18, of which waited for: 9 -> 10; matrix products, arithmetic and copies ran while one was open for 9% -> 9% of each run, Pallas kernels for 27% -> 22%
where the time goes in v3:
time: 171 us; the launch traced here: 169 us
  waiting for transfers between devices  62.5 us (37%)
  Pallas kernels  40.8 us (24%)
  starting transfers between devices  35.7 us (21%)
  local copies, waits for them, and re-layouts  17.5 us (10%)
  other arithmetic  11.9 us (7%)
    all_to_all x1, waiting for transfers between devices, body(): pieces1 = lax.all_to_all(sent1_16, 'vert', 0, 0, tiled=True)  16.5 us
    ppermute x1, waiting for transfers between devices, body(): theirs1 = lax.ppermute(theirs1, 'ia', X_HI)  13.8 us
    unnamed x44, local copies, waits for them, and re-layouts  12.1 us
    pallas_call x2, Pallas kernels, product_near(): pl.pallas_call(near_body, out_shape=out, grid_spec=pltpu.PrefetchScalarGr...  11.6 us
    pallas_call x2, Pallas kernels, turn_slabs(): pl.pallas_call(turn_body, out_shape=jax.ShapeDtypeStruct((size, count * s...  9.89 us
    ppermute x1, waiting for transfers between devices, body(): up = lax.ppermute(right, 'ia', y_ring(1))  8.74 us
    all_to_all x1, starting transfers between devices, body(): pieces0 = lax.all_to_all(sent0, 'vert', 0, 0, tiled=True)  8.19 us
    pallas_call x4, Pallas kernels, product(): pl.pallas_call(functools.partial(product_body, start), out_shape=out, gri...  6.7 us
  transfers between devices with their start and end apart: 18, of which 10 were waited for; matrix products, arithmetic and copies ran while one was open for 9% of the time, Pallas kernels for 22%

profile of v3, /device:TPU:1, one launch (start us, length us, event | category | flops | bytes accessed | tf_op | source)
XLA Modules:
  0.0 168.6 jit_solution(17590751226079182701)
XLA Ops:
  0.0 2.1 %collective-permute-start.1 = (bf16[640,1280]{1,0:T(8,128)(2,1)}, bf16[640,1280]{1,0:T(8,128)(2,1)S(1)}, u32[]{:S(2)}, u32[]{:S(2)}) collective-permute-start(bf16[640,1280]{1,0:T(8,128)(2,1)} %bitcast.12), channel_id=1, source_target_pairs={{0,32},{32,64},{64,96},{96,0},{128,160},{160,192},{192,224},{224,1... | collective-permute-start | bytes 4915208 | tf_op jit(solution)/shard_map/ppermute | solution.py:320
  4.8 3.9 %shard_map.64 = bf16[640,1280]{1,0:T(8,128)(2,1)} custom-call(s32[2]{0:T(128)} %slice_add_fusion.index, bf16[10,64,5120]{2,1,0:T(8,128)(2,1)} %u.2), custom_call_target="tpu_custom_call" | custom-call | flops 1000000000 | bytes 3000000 | tf_op jit(solution)/shard_map/pallas_call | solution.py:42
  8.7 2.5 %collective-permute-start = (bf16[640,1280]{1,0:T(8,128)(2,1)}, bf16[640,1280]{1,0:T(8,128)(2,1)S(1)}, u32[]{:S(2)}, u32[]{:S(2)}) collective-permute-start(bf16[640,1280]{1,0:T(8,128)(2,1)} %shard_map.64), channel_id=1, source_target_pairs={{0,144},{8,152},{16,128},{24,136},{32,176},{40,184},{48,160},{56,1... | collective-permute-start | bytes 4915208 | tf_op jit(solution)/shard_map/ppermute | solution.py:326
  13.4 6.0 %shard_map.65.near.far = bf16[640,2560]{1,0:T(8,128)(2,1)} custom-call(s32[4]{0:T(128)} %get-tuple-element.84.index, bf16[10,64,5120]{2,1,0:T(8,128)(2,1)} %u.2), custom_call_target="tpu_custom_call" | custom-call | flops 2000000000 | bytes 6000000 | tf_op jit(solution)/shard_map/pallas_call | solution.py:42
  22.5 4.5 %shard_map.66.w = bf16[200,6400]{1,0:T(8,128)(2,1)S(1)} custom-call(bf16[10,20,6400]{2,1,0:T(8,128)(2,1)S(1)} %copy-done.9, bf16[640,640]{1,0:T(8,128)(2,1)S(1)} %copy-done.8), custom_call_target="tpu_custom_call" | custom-call | flops 1000000000 | bytes 3000000 | tf_op jit(solution)/shard_map/pallas_call | solution.py:176
  28.5 8.7 %collective-permute-done.1.v3 = bf16[640,1280]{1,0:T(8,128)(2,1)S(1)} collective-permute-done((bf16[640,1280]{1,0:T(8,128)(2,1)}, bf16[640,1280]{1,0:T(8,128)(2,1)S(1)}, u32[]{:S(2)}, u32[]{:S(2)}) %collective-permute-start.1) | collective-permute-done | bytes 1638432 | tf_op jit(solution)/shard_map/ppermute | solution.py:320
  38.6 5.9 %shard_map.67.partial_sum = f32[640,1280]{1,0:T(8,128)S(1)} custom-call(s32[1]{0:T(128)} %constant.119.clone.1.place, bf16[640,2560]{1,0:T(8,128)(2,1)S(1)} %copy-done, bf16[640,2560]{1,0:T(8,128)(2,1)S(1)} %copy-done, bf16[640,1280]{1,0:T(8,128)(2,1)S(1)} %bitcast.14, bf16[640,1280]{1,0:T(8,128)(2,1)} %collective-permute-done.2.v1, ...), custom_call_target="tpu_custom_call" | custom-call | flops 1000000000 | bytes 3000000 | tf_op jit(solution)/shard_map/pallas_call | solution.py:83
  45.4 2.9 %collective-permute-start.4 = (bf16[640,1280]{1,0:T(8,128)(2,1)S(1)}, bf16[640,1280]{1,0:T(8,128)(2,1)S(1)}, u32[]{:S(2)}, u32[]{:S(2)}) collective-permute-start(bf16[640,1280]{1,0:T(8,128)(2,1)S(1)} %collective-permute-done.near), channel_id=1, source_target_pairs={{0,8},{8,0},{16,24},{24,16},{1,9},{9,1},{17,25},{25,17},{2,10},{10... | collective-permute-start | bytes 4915208 | tf_op jit(solution)/shard_map/ppermute | solution.py:338
  49.7 2.7 %collective-permute-start.8 = (bf16[320,1280]{1,0:T(8,128)(2,1)S(1)}, bf16[320,1280]{1,0:T(8,128)(2,1)S(1)}, u32[]{:S(2)}, u32[]{:S(2)}) collective-permute-start(bf16[320,1280]{1,0:T(8,128)(2,1)S(1)} %slice.23), channel_id=1, source_target_pairs={{0,96},{32,0},{64,32},{96,64},{128,224},{160,128},{192,160},{224,1... | collective-permute-start | bytes 2457608 | tf_op jit(solution)/shard_map/ppermute | solution.py:334
  54.8 5.7 %shard_map.68.partial_sum = f32[640,1280]{1,0:T(8,128)S(1)} custom-call(s32[1]{0:T(128)} %bitcast.1.place, bf16[640,1280]{1,0:T(8,128)(2,1)S(1)} %collective-permute-done.near, bf16[640,1280]{1,0:T(8,128)(2,1)S(1)} %collective-permute-done.4.far, bf16[640,1280]{1,0:T(8,128)(2,1)S(1)} %bitcast.15, bf16[640,1280]{1,0:T(8,128)(2,1)} %collective-permute-done.2.v1, ...), custom_call_target="tpu_custom_call" | custom-call | flops 1000000000 | bytes 3000000 | tf_op jit(solution)/shard_map/pallas_call | solution.py:83
  60.5 4.7 %collective-permute-done.6 = bf16[200,512]{1,0:T(8,128)(2,1)S(1)} collective-permute-done((bf16[200,512]{1,0:T(8,128)(2,1)S(1)}, bf16[200,512]{1,0:T(8,128)(2,1)S(1)}, u32[]{:S(2)}, u32[]{:S(2)}) %collective-permute-start.6) | collective-permute-done | bytes 204832 | tf_op jit(solution)/shard_map/ppermute | solution.py:324
  66.9 3.9 %collective-permute-done.7.v2a = bf16[320,1280]{1,0:T(8,128)(2,1)S(1)} collective-permute-done((bf16[320,1280]{1,0:T(8,128)(2,1)S(1)}, bf16[320,1280]{1,0:T(8,128)(2,1)S(1)}, u32[]{:S(2)}, u32[]{:S(2)}) %collective-permute-start.7) | collective-permute-done | bytes 819232 | tf_op jit(solution)/shard_map/ppermute | solution.py:333
  74.6 2.0 %shard_map.71 = f32[8,80,896]{2,1,0:T(8,128)S(1)} custom-call(s32[1]{0:T(128)} %constant.119.clone.1.place, f32[640,1280]{1,0:T(8,128)S(1)} %shard_map.67.partial_sum, bf16[640,2560]{1,0:T(8,128)(2,1)S(1)} %copy-done, bf16[640,2560]{1,0:T(8,128)(2,1)S(1)} %copy-done, bf16[320,1280]{1,0:T(8,128)(2,1)S(1)} %collective-permute-done.7.v2a, ...), custom_call_target="tpu_custom_call" | custom-call | flops 1000000000 | bytes 3000000 | tf_op jit(solution)/shard_map/pallas_call | solution.py:132
  81.3 5.9 %collective-permute-done.10.down = bf16[4,200,512]{2,1,0:T(8,128)(2,1)S(1)} collective-permute-done((bf16[4,200,512]{2,1,0:T(8,128)(2,1)S(1)}, bf16[4,200,512]{2,1,0:T(8,128)(2,1)S(1)}, u32[]{:S(2)}, u32[]{:S(2)}) %collective-permute-start.10) | collective-permute-done | bytes 819232 | tf_op jit(solution)/shard_map/ppermute | solution.py:344
  92.1 2.1 %collective-permute-start.13 = (bf16[2,200,512]{2,1,0:T(8,128)(2,1)}, bf16[2,200,512]{2,1,0:T(8,128)(2,1)S(1)}, u32[]{:S(2)}, u32[]{:S(2)}) collective-permute-start(bf16[2,200,512]{2,1,0:T(8,128)(2,1)} %slice.25), channel_id=1, source_target_pairs={{0,96},{32,0},{64,32},{96,64},{128,224},{160,128},{192,160},{224,1... | collective-permute-start | bytes 1228808 | tf_op jit(solution)/shard_map/ppermute | solution.py:362
  94.1 8.2 %all-to-all-start.1 = ((f16[8,160,384]{2,1,0:T(8,128)(2,1)}), f16[8,160,384]{2,1,0:T(8,128)(2,1)}, u32[]{:S(2)}, u32[]{:S(2)}) async-start(f16[8,160,384]{2,1,0:T(8,128)(2,1)} %fusion), calls=%async_computation.1 | async-start | bytes 1966080 | tf_op jit(solution)/shard_map/all_to_all | solution.py:352
  102.3 13.8 %collective-permute-done.11 = f16[8,80,896]{2,1,0:T(8,128)(2,1)} collective-permute-done((f16[8,80,896]{2,1,0:T(8,128)(2,1)}, f16[8,80,896]{2,1,0:T(8,128)(2,1)}, u32[]{:S(2)}, u32[]{:S(2)}) %collective-permute-start.11) | collective-permute-done | bytes 1146912 | tf_op jit(solution)/shard_map/ppermute | solution.py:360
  116.1 2.7 %add_convert_fusion = f16[8,80,896]{2,1,0:T(8,128)(2,1)} fusion(f16[8,80,896]{2,1,0:T(8,128)(2,1)} %collective-permute-done.11, f32[8,80,896]{2,1,0:T(8,128)S(1)} %copy-done.4), kind=kLoop, calls=%fused_computation.1 | loop fusion | flops 2293760 | bytes 4587520 | tf_op jit(solution)/shard_map/convert_element_type | solution.py:363
  124.4 5.8 %all-to-all-done.1 = f16[8,160,384]{2,1,0:T(8,128)(2,1)} async-done(((f16[8,160,384]{2,1,0:T(8,128)(2,1)}), f16[8,160,384]{2,1,0:T(8,128)(2,1)}, u32[]{:S(2)}, u32[]{:S(2)}) %all-to-all-start.1) | async-done | bytes 983072 | tf_op jit(solution)/shard_map/all_to_all | solution.py:352
  130.2 4.3 %all-to-all-start = ((f16[8,80,896]{2,1,0:T(8,128)(2,1)}), f16[8,80,896]{2,1,0:T(8,128)(2,1)}, u32[]{:S(2)}, u32[]{:S(2)}) async-start(f16[8,80,896]{2,1,0:T(8,128)(2,1)} %add_convert_fusion), calls=%async_computation | async-start | bytes 2293760 | tf_op jit(solution)/shard_map/all_to_all | solution.py:364
  141.3 5.0 %shard_map.74.ladder = f32[10,20,512]{2,1,0:T(8,128)S(1)} custom-call(s32[3]{0:T(128)S(1)} %pad_add_fusion.1.place, bf16[200,6400]{1,0:T(8,128)(2,1)S(1)} %copy-done.2, bf16[4,800,512]{2,1,0:T(8,128)(2,1)S(1)} %bitcast.11, bf16[4,800,512]{2,1,0:T(8,128)(2,1)} %collective-permute-done.14.far), custom_call_target="tpu_custom_call" | custom-call | flops 1000000000 | bytes 3000000 | tf_op jit(solution)/shard_map/pallas_call | solution.py:252
  147.1 16.5 %all-to-all-done = f16[8,80,896]{2,1,0:T(8,128)(2,1)} async-done(((f16[8,80,896]{2,1,0:T(8,128)(2,1)}), f16[8,80,896]{2,1,0:T(8,128)(2,1)}, u32[]{:S(2)}, u32[]{:S(2)}) %all-to-all-start) | async-done | bytes 1146912 | tf_op jit(solution)/shard_map/all_to_all | solution.py:364
  163.6 2.2 %convert_reduce_fusion.sum1 = f32[80,896]{1,0:T(8,128)} fusion(f16[8,80,896]{2,1,0:T(8,128)(2,1)} %all-to-all-done), kind=kLoop, calls=%fused_computation | loop fusion | flops 1075200 | bytes 1433600 | tf_op jit(solution)/shard_map/reduce_sum | solution.py:382
  165.8 2.9 %shard_map.75 = bf16[10,20,512]{2,1,0:T(8,128)(2,1)} custom-call(s32[10]{0:T(128)} %dynamic_slice.16.sym_i, f32[80,384]{1,0:T(8,128)} %get-tuple-element.81.sum0, f32[80,384]{1,0:T(8,128)} %copy-done.20, f32[80,896]{1,0:T(8,128)} %convert_reduce_fusion.sum1, f32[10,20,512]{2,1,0:T(8,128)} %copy-done.14, s32[20,512]{1,0:T(8,128)} %broadcast_xor_fusion.table), custom_call_target="tpu_custom_call" | custom-call | flops 1000000000 | bytes 3000000 | tf_op jit(solution)/shard_map/pallas_call | solution.py:293
  (93 shorter events, 43.7 us)
Async XLA Ops:
  0.0 37.2 %collective-permute-start.1 = (bf16[640,1280]{1,0:T(8,128)(2,1)}, bf16[640,1280]{1,0:T(8,128)(2,1)S(1)}, u32[]{:S(2)}, u32[]{:S(2)}) collective-permute-start(bf16[640,1280]{1,0:T(8,128)(2,1)} %bitcast.12), channel_id=1, source_target_pairs={{0,32},{32,64},{64,96},{96,0},{128,160},{160,192},{192,224},{224,1... | collective-permute-start | bytes 4915208 | tf_op jit(solution)/shard_map/ppermute | solution.py:320
  2.1 36.5 %collective-permute-start.2 = (bf16[640,1280]{1,0:T(8,128)(2,1)}, bf16[640,1280]{1,0:T(8,128)(2,1)}, u32[]{:S(2)}, u32[]{:S(2)}) collective-permute-start(bf16[640,1280]{1,0:T(8,128)(2,1)} %bitcast.13), channel_id=1, source_target_pairs={{0,96},{32,0},{64,32},{96,64},{128,224},{160,128},{192,160},{224,1... | collective-permute-start | bytes 4915208 | tf_op jit(solution)/shard_map/ppermute | solution.py:321
  8.7 36.7 %collective-permute-start = (bf16[640,1280]{1,0:T(8,128)(2,1)}, bf16[640,1280]{1,0:T(8,128)(2,1)S(1)}, u32[]{:S(2)}, u32[]{:S(2)}) collective-permute-start(bf16[640,1280]{1,0:T(8,128)(2,1)} %shard_map.64), channel_id=1, source_target_pairs={{0,144},{8,152},{16,128},{24,136},{32,176},{40,184},{48,160},{56,1... | collective-permute-start | bytes 4915208 | tf_op jit(solution)/shard_map/ppermute | solution.py:326
  12.2 26.5 %collective-permute-start.3 = (bf16[200,512]{1,0:T(8,128)(2,1)S(1)}, bf16[200,512]{1,0:T(8,128)(2,1)S(1)}, u32[]{:S(2)}, u32[]{:S(2)}) collective-permute-start(bf16[200,512]{1,0:T(8,128)(2,1)S(1)} %reshape.68), channel_id=1, source_target_pairs={{0,16},{8,24},{16,0},{24,8},{1,17},{9,25},{17,1},{25,9},{2,18},{10... | collective-permute-start | bytes 614408 | tf_op jit(solution)/shard_map/ppermute | solution.py:323
  22.5 16.1 %copy-start.5 = (bf16[10,64,1280]{2,1,0:T(8,128)(2,1)S(1)}, bf16[10,64,1280]{2,1,0:T(8,128)(2,1)}, u32[]{:S(2)}) copy-start(bf16[10,64,1280]{2,1,0:T(8,128)(2,1)} %param.9) | copy-start | bytes 4915204
  45.4 9.4 %collective-permute-start.4 = (bf16[640,1280]{1,0:T(8,128)(2,1)S(1)}, bf16[640,1280]{1,0:T(8,128)(2,1)S(1)}, u32[]{:S(2)}, u32[]{:S(2)}) collective-permute-start(bf16[640,1280]{1,0:T(8,128)(2,1)S(1)} %collective-permute-done.near), channel_id=1, source_target_pairs={{0,8},{8,0},{16,24},{24,16},{1,9},{9,1},{17,25},{25,17},{2,10},{10... | collective-permute-start | bytes 4915208 | tf_op jit(solution)/shard_map/ppermute | solution.py:338
  49.6 21.2 %collective-permute-start.7 = (bf16[320,1280]{1,0:T(8,128)(2,1)S(1)}, bf16[320,1280]{1,0:T(8,128)(2,1)S(1)}, u32[]{:S(2)}, u32[]{:S(2)}) collective-permute-start(bf16[320,1280]{1,0:T(8,128)(2,1)S(1)} %slice.22), channel_id=1, source_target_pairs={{0,32},{32,64},{64,96},{96,0},{128,160},{160,192},{192,224},{224,1... | collective-permute-start | bytes 2457608 | tf_op jit(solution)/shard_map/ppermute | solution.py:333
  49.7 21.1 %collective-permute-start.8 = (bf16[320,1280]{1,0:T(8,128)(2,1)S(1)}, bf16[320,1280]{1,0:T(8,128)(2,1)S(1)}, u32[]{:S(2)}, u32[]{:S(2)}) collective-permute-start(bf16[320,1280]{1,0:T(8,128)(2,1)S(1)} %slice.23), channel_id=1, source_target_pairs={{0,96},{32,0},{64,32},{96,64},{128,224},{160,128},{192,160},{224,1... | collective-permute-start | bytes 2457608 | tf_op jit(solution)/shard_map/ppermute | solution.py:334
  52.3 8.2 %collective-permute-start.5 = (bf16[200,512]{1,0:T(8,128)(2,1)S(1)}, bf16[200,512]{1,0:T(8,128)(2,1)S(1)}, u32[]{:S(2)}, u32[]{:S(2)}) collective-permute-start(bf16[200,512]{1,0:T(8,128)(2,1)S(1)} %reshape.68), channel_id=1, source_target_pairs={{0,128},{32,160},{64,192},{96,224},{128,0},{160,32},{192,64},{224,... | collective-permute-start | bytes 614408 | tf_op jit(solution)/shard_map/ppermute | solution.py:323
  53.9 11.4 %collective-permute-start.6 = (bf16[200,512]{1,0:T(8,128)(2,1)S(1)}, bf16[200,512]{1,0:T(8,128)(2,1)S(1)}, u32[]{:S(2)}, u32[]{:S(2)}) collective-permute-start(bf16[200,512]{1,0:T(8,128)(2,1)S(1)} %reshape.68), channel_id=1, source_target_pairs={{0,144},{8,152},{16,128},{24,136},{32,176},{40,184},{48,160},{56,1... | collective-permute-start | bytes 614408 | tf_op jit(solution)/shard_map/ppermute | solution.py:324
  65.3 21.9 %collective-permute-start.10 = (bf16[4,200,512]{2,1,0:T(8,128)(2,1)S(1)}, bf16[4,200,512]{2,1,0:T(8,128)(2,1)S(1)}, u32[]{:S(2)}, u32[]{:S(2)}) collective-permute-start(bf16[4,200,512]{2,1,0:T(8,128)(2,1)S(1)} %pad_maximum_fusion.own), channel_id=1, source_target_pairs={{0,96},{32,0},{64,32},{96,64},{128,224},{160,128},{192,160},{224,1... | collective-permute-start | bytes 2457608 | tf_op jit(solution)/shard_map/ppermute | solution.py:344
  65.7 22.6 %collective-permute-start.9 = (bf16[4,200,512]{2,1,0:T(8,128)(2,1)S(1)}, bf16[4,200,512]{2,1,0:T(8,128)(2,1)S(1)}, u32[]{:S(2)}, u32[]{:S(2)}) collective-permute-start(bf16[4,200,512]{2,1,0:T(8,128)(2,1)S(1)} %pad_maximum_fusion.own), channel_id=1, source_target_pairs={{0,32},{32,64},{64,96},{96,0},{128,160},{160,192},{192,224},{224,1... | collective-permute-start | bytes 2457608 | tf_op jit(solution)/shard_map/ppermute | solution.py:343
  81.3 34.8 %copy-start.4 = (f32[8,80,896]{2,1,0:T(8,128)S(1)}, f32[8,80,896]{2,1,0:T(8,128)}, u32[]{:S(2)}) copy-start(f32[8,80,896]{2,1,0:T(8,128)} %copy-done.3) | copy-start | bytes 6881284
  88.3 27.8 %collective-permute-start.11 = (f16[8,80,896]{2,1,0:T(8,128)(2,1)}, f16[8,80,896]{2,1,0:T(8,128)(2,1)}, u32[]{:S(2)}, u32[]{:S(2)}) collective-permute-start(f16[8,80,896]{2,1,0:T(8,128)(2,1)} %multiply_convert_fusion), channel_id=1, source_target_pairs={{0,128},{32,160},{64,192},{96,224},{128,0},{160,32},{192,64},{224,... | collective-permute-start | bytes 3440648 | tf_op jit(solution)/shard_map/ppermute | solution.py:360
  90.6 28.2 %collective-permute-start.12 = (bf16[2,200,512]{2,1,0:T(8,128)(2,1)}, bf16[2,200,512]{2,1,0:T(8,128)(2,1)S(1)}, u32[]{:S(2)}, u32[]{:S(2)}) collective-permute-start(bf16[2,200,512]{2,1,0:T(8,128)(2,1)} %slice.24), channel_id=1, source_target_pairs={{0,32},{32,64},{64,96},{96,0},{128,160},{160,192},{192,224},{224,1... | collective-permute-start | bytes 1228808 | tf_op jit(solution)/shard_map/ppermute | solution.py:361
  92.1 27.6 %collective-permute-start.13 = (bf16[2,200,512]{2,1,0:T(8,128)(2,1)}, bf16[2,200,512]{2,1,0:T(8,128)(2,1)S(1)}, u32[]{:S(2)}, u32[]{:S(2)}) collective-permute-start(bf16[2,200,512]{2,1,0:T(8,128)(2,1)} %slice.25), channel_id=1, source_target_pairs={{0,96},{32,0},{64,32},{96,64},{128,224},{160,128},{192,160},{224,1... | collective-permute-start | bytes 1228808 | tf_op jit(solution)/shard_map/ppermute | solution.py:362
  94.1 36.1 %all-to-all-start.1 = ((f16[8,160,384]{2,1,0:T(8,128)(2,1)}), f16[8,160,384]{2,1,0:T(8,128)(2,1)}, u32[]{:S(2)}, u32[]{:S(2)}) async-start(f16[8,160,384]{2,1,0:T(8,128)(2,1)} %fusion), calls=%async_computation.1 | async-start | bytes 1966080 | tf_op jit(solution)/shard_map/all_to_all | solution.py:352
  102.3 18.1 %copy-start.7 = (bf16[4,200,512]{2,1,0:T(8,128)(2,1)S(1)}, bf16[4,200,512]{2,1,0:T(8,128)(2,1)}, u32[]{:S(2)}) copy-start(bf16[4,200,512]{2,1,0:T(8,128)(2,1)} %copy-done.6) | copy-start | bytes 2457604
  102.3 18.1 %copy-start.11 = (bf16[4,200,512]{2,1,0:T(8,128)(2,1)S(1)}, bf16[4,200,512]{2,1,0:T(8,128)(2,1)}, u32[]{:S(2)}) copy-start(bf16[4,200,512]{2,1,0:T(8,128)(2,1)} %copy-done.10) | copy-start | bytes 2457604
  102.3 18.1 %copy-start.13 = (bf16[4,200,512]{2,1,0:T(8,128)(2,1)S(1)}, bf16[4,200,512]{2,1,0:T(8,128)(2,1)}, u32[]{:S(2)}) copy-start(bf16[4,200,512]{2,1,0:T(8,128)(2,1)} %copy-done.12) | copy-start | bytes 2457604
  122.7 16.9 %collective-permute-start.14 = (bf16[4,800,512]{2,1,0:T(8,128)(2,1)S(1)}, bf16[4,800,512]{2,1,0:T(8,128)(2,1)}, u32[]{:S(2)}, u32[]{:S(2)}) collective-permute-start(bf16[4,800,512]{2,1,0:T(8,128)(2,1)S(1)} %bitcast.10), channel_id=1, source_target_pairs={{0,8},{8,0},{16,24},{24,16},{1,9},{9,1},{17,25},{25,17},{2,10},{10... | collective-permute-start | bytes 9830408 | tf_op jit(solution)/shard_map/ppermute | solution.py:368
  130.2 33.4 %all-to-all-start = ((f16[8,80,896]{2,1,0:T(8,128)(2,1)}), f16[8,80,896]{2,1,0:T(8,128)(2,1)}, u32[]{:S(2)}, u32[]{:S(2)}) async-start(f16[8,80,896]{2,1,0:T(8,128)(2,1)} %add_convert_fusion), calls=%async_computation | async-start | bytes 2293760 | tf_op jit(solution)/shard_map/all_to_all | solution.py:364
  137.5 9.6 %collective-permute-start.15 = (f32[80,384]{1,0:T(8,128)S(1)}, f32[80,384]{1,0:T(8,128)S(1)}, u32[]{:S(2)}, u32[]{:S(2)}) collective-permute-start(f32[80,384]{1,0:T(8,128)S(1)} %get-tuple-element.82), channel_id=1, source_target_pairs={{0,128},{32,160},{64,192},{96,224},{128,0},{160,32},{192,64},{224,... | collective-permute-start | bytes 368648 | tf_op jit(solution)/shard_map/ppermute | solution.py:374
  147.1 18.6 %copy-start.20 = (f32[80,384]{1,0:T(8,128)}, f32[80,384]{1,0:T(8,128)S(1)}, u32[]{:S(2)}) copy-start(f32[80,384]{1,0:T(8,128)S(1)} %collective-permute-done.15.other0) | copy-start | bytes 368644
  (16 other events, 66.5 us)

commit v4 on v3

--- a/solution.py
+++ b/solution.py
@@ -333,7 +333,7 @@
     v2a = lax.ppermute(up[:half], "ia", y_ring(1))
     v2b = lax.ppermute(down[half:], "ia", y_ring(-1))
     flat = jnp.zeros_like(z)
-    ours = product_near(flat, (left,), (right, down, up), tx[1])
+    ours = product_near(flat, (left,), (right, down, up), tx[1], got)
     got, ours = after(got, ours)
     got_core = lax.ppermute(got, "ja", CORE)
     theirs = product_near(core, (got, got_core), (right, down, up))

time: 171 us -> 177 us (1.035)
  waiting for transfers between devices: 62.5 us -> 68.4 us
    ppermute x1, waiting for transfers between devices: 0.87 us -> 6.78 us  [body(): got = lax.ppermute(mine, ('ia', 'ja'), X_CROSS)]
  transfers between devices with their start and end apart: 18 -> 18, of which waited for: 10 -> 10; matrix products, arithmetic and copies ran while one was open for 9% -> 9% of each run, Pallas kernels for 22% -> 18%
where the time goes in v4:
time: 177 us; the launch traced here: 175 us
  waiting for transfers between devices  68.4 us (39%)
  Pallas kernels  40.8 us (23%)
  starting transfers between devices  35.8 us (20%)
  local copies, waits for them, and re-layouts  17.5 us (10%)
  other arithmetic  11.9 us (7%)
    all_to_all x1, waiting for transfers between devices, body(): pieces1 = lax.all_to_all(sent1_16, 'vert', 0, 0, tiled=True)  16.5 us
    ppermute x1, waiting for transfers between devices, body(): theirs1 = lax.ppermute(theirs1, 'ia', X_HI)  13.8 us
    unnamed x44, local copies, waits for them, and re-layouts  12.1 us
    pallas_call x2, Pallas kernels, product_near(): pl.pallas_call(near_body, out_shape=out, grid_spec=pltpu.PrefetchScalarGr...  11.6 us
    pallas_call x2, Pallas kernels, turn_slabs(): pl.pallas_call(turn_body, out_shape=jax.ShapeDtypeStruct((size, count * s...  9.89 us
    ppermute x1, waiting for transfers between devices, body(): up = lax.ppermute(right, 'ia', y_ring(1))  8.74 us
    all_to_all x1, starting transfers between devices, body(): pieces0 = lax.all_to_all(sent0, 'vert', 0, 0, tiled=True)  8.18 us
    ppermute x1, waiting for transfers between devices, body(): got = lax.ppermute(mine, ('ia', 'ja'), X_CROSS)  6.78 us
  transfers between devices with their start and end apart: 18, of which 10 were waited for; matrix products, arithmetic and copies ran while one was open for 9% of the time, Pallas kernels for 18%

profile of v4, /device:TPU:1, one launch (start us, length us, event | category | flops | bytes accessed | tf_op | source)
XLA Modules:
  0.0 174.6 jit_solution(1951097423214293676)
XLA Ops:
  0.0 2.1 %collective-permute-start.1 = (bf16[640,1280]{1,0:T(8,128)(2,1)}, bf16[640,1280]{1,0:T(8,128)(2,1)S(1)}, u32[]{:S(2)}, u32[]{:S(2)}) collective-permute-start(bf16[640,1280]{1,0:T(8,128)(2,1)} %bitcast.12), channel_id=1, source_target_pairs={{0,32},{32,64},{64,96},{96,0},{128,160},{160,192},{192,224},{224,1... | collective-permute-start | bytes 4915208 | tf_op jit(solution)/shard_map/ppermute | solution.py:320
  4.8 3.9 %shard_map.64 = bf16[640,1280]{1,0:T(8,128)(2,1)} custom-call(s32[2]{0:T(128)} %slice_add_fusion.index, bf16[10,64,5120]{2,1,0:T(8,128)(2,1)} %u.2), custom_call_target="tpu_custom_call" | custom-call | flops 1000000000 | bytes 3000000 | tf_op jit(solution)/shard_map/pallas_call | solution.py:42
  8.7 2.5 %collective-permute-start = (bf16[640,1280]{1,0:T(8,128)(2,1)}, bf16[640,1280]{1,0:T(8,128)(2,1)S(1)}, u32[]{:S(2)}, u32[]{:S(2)}) collective-permute-start(bf16[640,1280]{1,0:T(8,128)(2,1)} %shard_map.64), channel_id=1, source_target_pairs={{0,144},{8,152},{16,128},{24,136},{32,176},{40,184},{48,160},{56,1... | collective-permute-start | bytes 4915208 | tf_op jit(solution)/shard_map/ppermute | solution.py:326
  13.4 6.0 %shard_map.65.near.far = bf16[640,2560]{1,0:T(8,128)(2,1)} custom-call(s32[4]{0:T(128)} %get-tuple-element.84.index, bf16[10,64,5120]{2,1,0:T(8,128)(2,1)} %u.2), custom_call_target="tpu_custom_call" | custom-call | flops 2000000000 | bytes 6000000 | tf_op jit(solution)/shard_map/pallas_call | solution.py:42
  22.5 4.5 %shard_map.66.w = bf16[200,6400]{1,0:T(8,128)(2,1)S(1)} custom-call(bf16[10,20,6400]{2,1,0:T(8,128)(2,1)S(1)} %copy-done.9, bf16[640,640]{1,0:T(8,128)(2,1)S(1)} %copy-done.8), custom_call_target="tpu_custom_call" | custom-call | flops 1000000000 | bytes 3000000 | tf_op jit(solution)/shard_map/pallas_call | solution.py:176
  28.5 8.7 %collective-permute-done.1.v3 = bf16[640,1280]{1,0:T(8,128)(2,1)S(1)} collective-permute-done((bf16[640,1280]{1,0:T(8,128)(2,1)}, bf16[640,1280]{1,0:T(8,128)(2,1)S(1)}, u32[]{:S(2)}, u32[]{:S(2)}) %collective-permute-start.1) | collective-permute-done | bytes 1638432 | tf_op jit(solution)/shard_map/ppermute | solution.py:320
  38.6 6.8 %collective-permute-done.refs_1_.near = bf16[640,1280]{1,0:T(8,128)(2,1)S(1)} collective-permute-done((bf16[640,1280]{1,0:T(8,128)(2,1)}, bf16[640,1280]{1,0:T(8,128)(2,1)S(1)}, u32[]{:S(2)}, u32[]{:S(2)}) %collective-permute-start) | collective-permute-done | bytes 1638432 | tf_op jit(solution)/shard_map/ppermute | solution.py:326
  45.4 5.9 %shard_map.67.partial_sum = f32[640,1280]{1,0:T(8,128)S(1)} custom-call(s32[1]{0:T(128)} %constant.119.clone.1.place, bf16[640,2560]{1,0:T(8,128)(2,1)S(1)} %copy-done, bf16[640,2560]{1,0:T(8,128)(2,1)S(1)} %copy-done, bf16[640,1280]{1,0:T(8,128)(2,1)S(1)} %bitcast.14, bf16[640,1280]{1,0:T(8,128)(2,1)} %collective-permute-done.2.v1, ...), custom_call_target="tpu_custom_call" | custom-call | flops 1000000000 | bytes 3000000 | tf_op jit(solution)/shard_map/pallas_call | solution.py:83
  51.3 3.0 %collective-permute-start.4 = (bf16[640,1280]{1,0:T(8,128)(2,1)S(1)}, bf16[640,1280]{1,0:T(8,128)(2,1)S(1)}, u32[]{:S(2)}, u32[]{:S(2)}) collective-permute-start(bf16[640,1280]{1,0:T(8,128)(2,1)S(1)} %collective-permute-done.refs_1_.near), channel_id=1, source_target_pairs={{0,8},{8,0},{16,24},{24,16},{1,9},{9,1},{17,25},{25,17},{2,10},{10... | collective-permute-start | bytes 4915208 | tf_op jit(solution)/shard_map/ppermute | solution.py:338
  55.7 2.7 %collective-permute-start.8 = (bf16[320,1280]{1,0:T(8,128)(2,1)S(1)}, bf16[320,1280]{1,0:T(8,128)(2,1)S(1)}, u32[]{:S(2)}, u32[]{:S(2)}) collective-permute-start(bf16[320,1280]{1,0:T(8,128)(2,1)S(1)} %slice.23), channel_id=1, source_target_pairs={{0,96},{32,0},{64,32},{96,64},{128,224},{160,128},{192,160},{224,1... | collective-permute-start | bytes 2457608 | tf_op jit(solution)/shard_map/ppermute | solution.py:334
  60.8 5.7 %shard_map.68.partial_sum = f32[640,1280]{1,0:T(8,128)S(1)} custom-call(s32[1]{0:T(128)} %bitcast.1.place, bf16[640,1280]{1,0:T(8,128)(2,1)S(1)} %collective-permute-done.refs_1_.near, bf16[640,1280]{1,0:T(8,128)(2,1)S(1)} %collective-permute-done.4.far, bf16[640,1280]{1,0:T(8,128)(2,1)S(1)} %bitcast.15, bf16[640,1280]{1,0:T(8,128)(2,1)} %collective-permute-done.2.v1, ...), custom_call_target="tpu_custom_call" | custom-call | flops 1000000000 | bytes 3000000 | tf_op jit(solution)/shard_map/pallas_call | solution.py:83
  66.5 4.7 %collective-permute-done.6 = bf16[200,512]{1,0:T(8,128)(2,1)S(1)} collective-permute-done((bf16[200,512]{1,0:T(8,128)(2,1)S(1)}, bf16[200,512]{1,0:T(8,128)(2,1)S(1)}, u32[]{:S(2)}, u32[]{:S(2)}) %collective-permute-start.6) | collective-permute-done | bytes 204832 | tf_op jit(solution)/shard_map/ppermute | solution.py:324
  72.9 3.8 %collective-permute-done.7.v2a = bf16[320,1280]{1,0:T(8,128)(2,1)S(1)} collective-permute-done((bf16[320,1280]{1,0:T(8,128)(2,1)S(1)}, bf16[320,1280]{1,0:T(8,128)(2,1)S(1)}, u32[]{:S(2)}, u32[]{:S(2)}) %collective-permute-start.7) | collective-permute-done | bytes 819232 | tf_op jit(solution)/shard_map/ppermute | solution.py:333
  87.3 5.9 %collective-permute-done.10.down = bf16[4,200,512]{2,1,0:T(8,128)(2,1)S(1)} collective-permute-done((bf16[4,200,512]{2,1,0:T(8,128)(2,1)S(1)}, bf16[4,200,512]{2,1,0:T(8,128)(2,1)S(1)}, u32[]{:S(2)}, u32[]{:S(2)}) %collective-permute-start.10) | collective-permute-done | bytes 819232 | tf_op jit(solution)/shard_map/ppermute | solution.py:344
  97.5 2.6 %collective-permute-start.13 = (bf16[2,200,512]{2,1,0:T(8,128)(2,1)}, bf16[2,200,512]{2,1,0:T(8,128)(2,1)S(1)}, u32[]{:S(2)}, u32[]{:S(2)}) collective-permute-start(bf16[2,200,512]{2,1,0:T(8,128)(2,1)} %slice.25), channel_id=1, source_target_pairs={{0,96},{32,0},{64,32},{96,64},{128,224},{160,128},{192,160},{224,1... | collective-permute-start | bytes 1228808 | tf_op jit(solution)/shard_map/ppermute | solution.py:362
  100.1 8.2 %all-to-all-start.1 = ((f16[8,160,384]{2,1,0:T(8,128)(2,1)}), f16[8,160,384]{2,1,0:T(8,128)(2,1)}, u32[]{:S(2)}, u32[]{:S(2)}) async-start(f16[8,160,384]{2,1,0:T(8,128)(2,1)} %fusion), calls=%async_computation.1 | async-start | bytes 1966080 | tf_op jit(solution)/shard_map/all_to_all | solution.py:352
  108.3 13.8 %collective-permute-done.11 = f16[8,80,896]{2,1,0:T(8,128)(2,1)} collective-permute-done((f16[8,80,896]{2,1,0:T(8,128)(2,1)}, f16[8,80,896]{2,1,0:T(8,128)(2,1)}, u32[]{:S(2)}, u32[]{:S(2)}) %collective-permute-start.11) | collective-permute-done | bytes 1146912 | tf_op jit(solution)/shard_map/ppermute | solution.py:360
  122.1 2.7 %add_convert_fusion = f16[8,80,896]{2,1,0:T(8,128)(2,1)} fusion(f16[8,80,896]{2,1,0:T(8,128)(2,1)} %collective-permute-done.11, f32[8,80,896]{2,1,0:T(8,128)S(1)} %copy-done.4), kind=kLoop, calls=%fused_computation.1 | loop fusion | flops 2293760 | bytes 4587520 | tf_op jit(solution)/shard_map/convert_element_type | solution.py:363
  130.4 5.8 %all-to-all-done.1 = f16[8,160,384]{2,1,0:T(8,128)(2,1)} async-done(((f16[8,160,384]{2,1,0:T(8,128)(2,1)}), f16[8,160,384]{2,1,0:T(8,128)(2,1)}, u32[]{:S(2)}, u32[]{:S(2)}) %all-to-all-start.1) | async-done | bytes 983072 | tf_op jit(solution)/shard_map/all_to_all | solution.py:352
  136.2 4.3 %all-to-all-start = ((f16[8,80,896]{2,1,0:T(8,128)(2,1)}), f16[8,80,896]{2,1,0:T(8,128)(2,1)}, u32[]{:S(2)}, u32[]{:S(2)}) async-start(f16[8,80,896]{2,1,0:T(8,128)(2,1)} %add_convert_fusion), calls=%async_computation | async-start | bytes 2293760 | tf_op jit(solution)/shard_map/all_to_all | solution.py:364
  147.3 5.0 %shard_map.74.ladder = f32[10,20,512]{2,1,0:T(8,128)S(1)} custom-call(s32[3]{0:T(128)S(1)} %pad_add_fusion.1.place, bf16[200,6400]{1,0:T(8,128)(2,1)S(1)} %copy-done.2, bf16[4,800,512]{2,1,0:T(8,128)(2,1)S(1)} %bitcast.11, bf16[4,800,512]{2,1,0:T(8,128)(2,1)} %collective-permute-done.14.far), custom_call_target="tpu_custom_call" | custom-call | flops 1000000000 | bytes 3000000 | tf_op jit(solution)/shard_map/pallas_call | solution.py:252
  153.1 16.5 %all-to-all-done = f16[8,80,896]{2,1,0:T(8,128)(2,1)} async-done(((f16[8,80,896]{2,1,0:T(8,128)(2,1)}), f16[8,80,896]{2,1,0:T(8,128)(2,1)}, u32[]{:S(2)}, u32[]{:S(2)}) %all-to-all-start) | async-done | bytes 1146912 | tf_op jit(solution)/shard_map/all_to_all | solution.py:364
  169.6 2.2 %convert_reduce_fusion.sum1 = f32[80,896]{1,0:T(8,128)} fusion(f16[8,80,896]{2,1,0:T(8,128)(2,1)} %all-to-all-done), kind=kLoop, calls=%fused_computation | loop fusion | flops 1075200 | bytes 1433600 | tf_op jit(solution)/shard_map/reduce_sum | solution.py:382
  171.7 2.9 %shard_map.75 = bf16[10,20,512]{2,1,0:T(8,128)(2,1)} custom-call(s32[10]{0:T(128)} %dynamic_slice.16.sym_i, f32[80,384]{1,0:T(8,128)} %get-tuple-element.81.sum0, f32[80,384]{1,0:T(8,128)} %copy-done.20, f32[80,896]{1,0:T(8,128)} %convert_reduce_fusion.sum1, f32[10,20,512]{2,1,0:T(8,128)} %copy-done.14, s32[20,512]{1,0:T(8,128)} %broadcast_xor_fusion.table), custom_call_target="tpu_custom_call" | custom-call | flops 1000000000 | bytes 3000000 | tf_op jit(solution)/shard_map/pallas_call | solution.py:293
  (93 shorter events, 44.4 us)
Async XLA Ops:
  0.0 37.2 %collective-permute-start.1 = (bf16[640,1280]{1,0:T(8,128)(2,1)}, bf16[640,1280]{1,0:T(8,128)(2,1)S(1)}, u32[]{:S(2)}, u32[]{:S(2)}) collective-permute-start(bf16[640,1280]{1,0:T(8,128)(2,1)} %bitcast.12), channel_id=1, source_target_pairs={{0,32},{32,64},{64,96},{96,0},{128,160},{160,192},{192,224},{224,1... | collective-permute-start | bytes 4915208 | tf_op jit(solution)/shard_map/ppermute | solution.py:320
  2.1 36.5 %collective-permute-start.2 = (bf16[640,1280]{1,0:T(8,128)(2,1)}, bf16[640,1280]{1,0:T(8,128)(2,1)}, u32[]{:S(2)}, u32[]{:S(2)}) collective-permute-start(bf16[640,1280]{1,0:T(8,128)(2,1)} %bitcast.13), channel_id=1, source_target_pairs={{0,96},{32,0},{64,32},{96,64},{128,224},{160,128},{192,160},{224,1... | collective-permute-start | bytes 4915208 | tf_op jit(solution)/shard_map/ppermute | solution.py:321
  8.7 36.7 %collective-permute-start = (bf16[640,1280]{1,0:T(8,128)(2,1)}, bf16[640,1280]{1,0:T(8,128)(2,1)S(1)}, u32[]{:S(2)}, u32[]{:S(2)}) collective-permute-start(bf16[640,1280]{1,0:T(8,128)(2,1)} %shard_map.64), channel_id=1, source_target_pairs={{0,144},{8,152},{16,128},{24,136},{32,176},{40,184},{48,160},{56,1... | collective-permute-start | bytes 4915208 | tf_op jit(solution)/shard_map/ppermute | solution.py:326
  12.2 26.5 %collective-permute-start.3 = (bf16[200,512]{1,0:T(8,128)(2,1)S(1)}, bf16[200,512]{1,0:T(8,128)(2,1)S(1)}, u32[]{:S(2)}, u32[]{:S(2)}) collective-permute-start(bf16[200,512]{1,0:T(8,128)(2,1)S(1)} %reshape.68), channel_id=1, source_target_pairs={{0,16},{8,24},{16,0},{24,8},{1,17},{9,25},{17,1},{25,9},{2,18},{10... | collective-permute-start | bytes 614408 | tf_op jit(solution)/shard_map/ppermute | solution.py:323
  22.5 22.9 %copy-start = (bf16[640,2560]{1,0:T(8,128)(2,1)S(1)}, bf16[640,2560]{1,0:T(8,128)(2,1)}, u32[]{:S(2)}) copy-start(bf16[640,2560]{1,0:T(8,128)(2,1)} %shard_map.65.near.far) | copy-start | bytes 9830404
  22.5 22.9 %copy-start.5 = (bf16[10,64,1280]{2,1,0:T(8,128)(2,1)S(1)}, bf16[10,64,1280]{2,1,0:T(8,128)(2,1)}, u32[]{:S(2)}) copy-start(bf16[10,64,1280]{2,1,0:T(8,128)(2,1)} %param.9) | copy-start | bytes 4915204
  51.3 9.5 %collective-permute-start.4 = (bf16[640,1280]{1,0:T(8,128)(2,1)S(1)}, bf16[640,1280]{1,0:T(8,128)(2,1)S(1)}, u32[]{:S(2)}, u32[]{:S(2)}) collective-permute-start(bf16[640,1280]{1,0:T(8,128)(2,1)S(1)} %collective-permute-done.refs_1_.near), channel_id=1, source_target_pairs={{0,8},{8,0},{16,24},{24,16},{1,9},{9,1},{17,25},{25,17},{2,10},{10... | collective-permute-start | bytes 4915208 | tf_op jit(solution)/shard_map/ppermute | solution.py:338
  55.6 21.1 %collective-permute-start.7 = (bf16[320,1280]{1,0:T(8,128)(2,1)S(1)}, bf16[320,1280]{1,0:T(8,128)(2,1)S(1)}, u32[]{:S(2)}, u32[]{:S(2)}) collective-permute-start(bf16[320,1280]{1,0:T(8,128)(2,1)S(1)} %slice.22), channel_id=1, source_target_pairs={{0,32},{32,64},{64,96},{96,0},{128,160},{160,192},{192,224},{224,1... | collective-permute-start | bytes 2457608 | tf_op jit(solution)/shard_map/ppermute | solution.py:333
  55.7 21.0 %collective-permute-start.8 = (bf16[320,1280]{1,0:T(8,128)(2,1)S(1)}, bf16[320,1280]{1,0:T(8,128)(2,1)S(1)}, u32[]{:S(2)}, u32[]{:S(2)}) collective-permute-start(bf16[320,1280]{1,0:T(8,128)(2,1)S(1)} %slice.23), channel_id=1, source_target_pairs={{0,96},{32,0},{64,32},{96,64},{128,224},{160,128},{192,160},{224,1... | collective-permute-start | bytes 2457608 | tf_op jit(solution)/shard_map/ppermute | solution.py:334
  58.3 8.2 %collective-permute-start.5 = (bf16[200,512]{1,0:T(8,128)(2,1)S(1)}, bf16[200,512]{1,0:T(8,128)(2,1)S(1)}, u32[]{:S(2)}, u32[]{:S(2)}) collective-permute-start(bf16[200,512]{1,0:T(8,128)(2,1)S(1)} %reshape.68), channel_id=1, source_target_pairs={{0,128},{32,160},{64,192},{96,224},{128,0},{160,32},{192,64},{224,... | collective-permute-start | bytes 614408 | tf_op jit(solution)/shard_map/ppermute | solution.py:323
  59.9 11.4 %collective-permute-start.6 = (bf16[200,512]{1,0:T(8,128)(2,1)S(1)}, bf16[200,512]{1,0:T(8,128)(2,1)S(1)}, u32[]{:S(2)}, u32[]{:S(2)}) collective-permute-start(bf16[200,512]{1,0:T(8,128)(2,1)S(1)} %reshape.68), channel_id=1, source_target_pairs={{0,144},{8,152},{16,128},{24,136},{32,176},{40,184},{48,160},{56,1... | collective-permute-start | bytes 614408 | tf_op jit(solution)/shard_map/ppermute | solution.py:324
  71.3 21.9 %collective-permute-start.10 = (bf16[4,200,512]{2,1,0:T(8,128)(2,1)S(1)}, bf16[4,200,512]{2,1,0:T(8,128)(2,1)S(1)}, u32[]{:S(2)}, u32[]{:S(2)}) collective-permute-start(bf16[4,200,512]{2,1,0:T(8,128)(2,1)S(1)} %pad_maximum_fusion.own), channel_id=1, source_target_pairs={{0,96},{32,0},{64,32},{96,64},{128,224},{160,128},{192,160},{224,1... | collective-permute-start | bytes 2457608 | tf_op jit(solution)/shard_map/ppermute | solution.py:344
  71.7 22.6 %collective-permute-start.9 = (bf16[4,200,512]{2,1,0:T(8,128)(2,1)S(1)}, bf16[4,200,512]{2,1,0:T(8,128)(2,1)S(1)}, u32[]{:S(2)}, u32[]{:S(2)}) collective-permute-start(bf16[4,200,512]{2,1,0:T(8,128)(2,1)S(1)} %pad_maximum_fusion.own), channel_id=1, source_target_pairs={{0,32},{32,64},{64,96},{96,0},{128,160},{160,192},{192,224},{224,1... | collective-permute-start | bytes 2457608 | tf_op jit(solution)/shard_map/ppermute | solution.py:343
  87.3 34.8 %copy-start.4 = (f32[8,80,896]{2,1,0:T(8,128)S(1)}, f32[8,80,896]{2,1,0:T(8,128)}, u32[]{:S(2)}) copy-start(f32[8,80,896]{2,1,0:T(8,128)} %copy-done.3) | copy-start | bytes 6881284
  94.3 27.8 %collective-permute-start.11 = (f16[8,80,896]{2,1,0:T(8,128)(2,1)}, f16[8,80,896]{2,1,0:T(8,128)(2,1)}, u32[]{:S(2)}, u32[]{:S(2)}) collective-permute-start(f16[8,80,896]{2,1,0:T(8,128)(2,1)} %multiply_convert_fusion), channel_id=1, source_target_pairs={{0,128},{32,160},{64,192},{96,224},{128,0},{160,32},{192,64},{224,... | collective-permute-start | bytes 3440648 | tf_op jit(solution)/shard_map/ppermute | solution.py:360
  96.6 28.2 %collective-permute-start.12 = (bf16[2,200,512]{2,1,0:T(8,128)(2,1)}, bf16[2,200,512]{2,1,0:T(8,128)(2,1)S(1)}, u32[]{:S(2)}, u32[]{:S(2)}) collective-permute-start(bf16[2,200,512]{2,1,0:T(8,128)(2,1)} %slice.24), channel_id=1, source_target_pairs={{0,32},{32,64},{64,96},{96,0},{128,160},{160,192},{192,224},{224,1... | collective-permute-start | bytes 1228808 | tf_op jit(solution)/shard_map/ppermute | solution.py:361
  97.5 28.1 %collective-permute-start.13 = (bf16[2,200,512]{2,1,0:T(8,128)(2,1)}, bf16[2,200,512]{2,1,0:T(8,128)(2,1)S(1)}, u32[]{:S(2)}, u32[]{:S(2)}) collective-permute-start(bf16[2,200,512]{2,1,0:T(8,128)(2,1)} %slice.25), channel_id=1, source_target_pairs={{0,96},{32,0},{64,32},{96,64},{128,224},{160,128},{192,160},{224,1... | collective-permute-start | bytes 1228808 | tf_op jit(solution)/shard_map/ppermute | solution.py:362
  100.1 36.1 %all-to-all-start.1 = ((f16[8,160,384]{2,1,0:T(8,128)(2,1)}), f16[8,160,384]{2,1,0:T(8,128)(2,1)}, u32[]{:S(2)}, u32[]{:S(2)}) async-start(f16[8,160,384]{2,1,0:T(8,128)(2,1)} %fusion), calls=%async_computation.1 | async-start | bytes 1966080 | tf_op jit(solution)/shard_map/all_to_all | solution.py:352
  108.3 18.1 %copy-start.7 = (bf16[4,200,512]{2,1,0:T(8,128)(2,1)S(1)}, bf16[4,200,512]{2,1,0:T(8,128)(2,1)}, u32[]{:S(2)}) copy-start(bf16[4,200,512]{2,1,0:T(8,128)(2,1)} %copy-done.6) | copy-start | bytes 2457604
  108.3 18.1 %copy-start.11 = (bf16[4,200,512]{2,1,0:T(8,128)(2,1)S(1)}, bf16[4,200,512]{2,1,0:T(8,128)(2,1)}, u32[]{:S(2)}) copy-start(bf16[4,200,512]{2,1,0:T(8,128)(2,1)} %copy-done.10) | copy-start | bytes 2457604
  128.6 16.9 %collective-permute-start.14 = (bf16[4,800,512]{2,1,0:T(8,128)(2,1)S(1)}, bf16[4,800,512]{2,1,0:T(8,128)(2,1)}, u32[]{:S(2)}, u32[]{:S(2)}) collective-permute-start(bf16[4,800,512]{2,1,0:T(8,128)(2,1)S(1)} %bitcast.10), channel_id=1, source_target_pairs={{0,8},{8,0},{16,24},{24,16},{1,9},{9,1},{17,25},{25,17},{2,10},{10... | collective-permute-start | bytes 9830408 | tf_op jit(solution)/shard_map/ppermute | solution.py:368
  136.2 33.4 %all-to-all-start = ((f16[8,80,896]{2,1,0:T(8,128)(2,1)}), f16[8,80,896]{2,1,0:T(8,128)(2,1)}, u32[]{:S(2)}, u32[]{:S(2)}) async-start(f16[8,80,896]{2,1,0:T(8,128)(2,1)} %add_convert_fusion), calls=%async_computation | async-start | bytes 2293760 | tf_op jit(solution)/shard_map/all_to_all | solution.py:364
  143.5 9.6 %collective-permute-start.15 = (f32[80,384]{1,0:T(8,128)S(1)}, f32[80,384]{1,0:T(8,128)S(1)}, u32[]{:S(2)}, u32[]{:S(2)}) collective-permute-start(f32[80,384]{1,0:T(8,128)S(1)} %get-tuple-element.82), channel_id=1, source_target_pairs={{0,128},{32,160},{64,192},{96,224},{128,0},{160,32},{192,64},{224,... | collective-permute-start | bytes 368648 | tf_op jit(solution)/shard_map/ppermute | solution.py:374
  153.1 18.6 %copy-start.20 = (f32[80,384]{1,0:T(8,128)}, f32[80,384]{1,0:T(8,128)S(1)}, u32[]{:S(2)}) copy-start(f32[80,384]{1,0:T(8,128)S(1)} %collective-permute-done.15.other0) | copy-start | bytes 368644
  (16 other events, 67.5 us)
